TPU v7x, 512 devices: a whole 4x8x8 slice. The times are simulated.
512 devices in a mesh: pipe: 16 (over x, z_hi, core), expert: 32 (over z_lo, y).
Axes of the slice: x: 4, y: 8, z: 8 (z_hi: 2, z_lo: 4; z = z_hi * 4 + z_lo), core: 2. Of those that a mesh axis runs over, the one named last changes fastest.
Arguments:
- fwd_in: bfloat16 [32768, 3584], P(('pipe', 'expert')), may hold values from -6 to 6
- fwd_routes: int32 [32768, 2], P(('pipe', 'expert')), may hold values from 0 to 3, all different within a row; in each aligned block of 64 rows (0 to 63, 64 to 127, ...) at most 34 rows name the same one
- router: bfloat16 [16, 3584, 4], P('pipe'), may hold values from -0.09375 to 0.09375
- bwd_in: bfloat16 [32768, 3584], P(('pipe', 'expert')), may hold values from -6 to 6
- bwd_routes: int32 [32768, 2], P(('pipe', 'expert')), may hold values from 0 to 3, all different within a row; in each aligned block of 64 rows (0 to 63, 64 to 127, ...) at most 34 rows name the same one
- bwd_gates: float32 [32768, 2], P(('pipe', 'expert')), may hold values from 0.1 to 0.9
- w_gate: bfloat16 [16, 3584, 4096], P('pipe', None, 'expert'), may hold values from -0.09375 to 0.09375
- w_up: bfloat16 [16, 3584, 4096], P('pipe', None, 'expert'), may hold values from -0.09375 to 0.09375
- w_down: bfloat16 [16, 4096, 3584], P('pipe', 'expert'), may hold values from -0.1875 to 0.1875
- saved_pre: bfloat16 [2, 16, 1088, 4096], P(None, 'pipe', None, 'expert'), may hold values from -5 to 5
Outputs:
- fwd_out: bfloat16 [32768, 3584], P(('pipe', 'expert'))
- bwd_out: bfloat16 [32768, 3584], P(('pipe', 'expert'))
Inputs may be any that keep to these rules, and one draw needn't show every extreme that they name: `fwd_routes`: in each device's 64 tokens (aligned blocks) no expert is named by more than 34 pairs, a bound that some block reaches; a token's experts differ. `bwd_routes`: as for fwd_routes.
All inputs are finite; a program needn't handle non-finite values.
Results may differ from a plain program's by a relative error of at most 0.0054.
Values may be sent and summed in bfloat16 or wider, within the bound.
No kernel may reach another device: no remote copies, remote signals or barrier semaphores. Data moves between devices by JAX's collectives and lax.ppermute only.
A program may use at most 128 MiB of HBM per device.

v0:
```python
import jax
import jax.numpy as jnp
from jax import lax
from jax.sharding import PartitionSpec as P

EXPERTS = 4
TOP = 2
CAP = 34


def shifted(array, axis, by):
    count = lax.axis_size(axis)
    return lax.ppermute(array, axis, [(i, (i + by) % count) for i in range(count)])


def slot_places(routes):
    rows = routes.shape[0]
    onehot = (routes[:, :, None] == jnp.arange(EXPERTS, dtype=jnp.int32)[None, None, :]).astype(
        jnp.int32
    )
    onehot = onehot.reshape(rows * TOP, EXPERTS)
    before = jnp.cumsum(onehot, axis=0) - onehot
    slot = jnp.sum(before * onehot, axis=1).reshape(rows, TOP)
    return routes * CAP + slot


def gather_rows(places, data):
    spots = jnp.arange(EXPERTS * CAP, dtype=jnp.int32)
    select = jnp.sum((places[None, :, :] == spots[:, None, None]).astype(jnp.float32), axis=2)
    return jnp.dot(select.astype(jnp.bfloat16), data, preferred_element_type=jnp.float32).astype(
        jnp.bfloat16
    )


def spread_back(places, weights, values):
    spots = jnp.arange(EXPERTS * CAP, dtype=jnp.int32)
    combine = jnp.sum(
        jnp.where(places[:, :, None] == spots[None, None, :], weights[:, :, None], 0.0), axis=1
    )
    return jnp.dot(combine, values, precision=lax.Precision.HIGHEST)


def lane_tree(terms):
    while terms.shape[1] > 1:
        half = terms.shape[1] // 2
        terms = lax.optimization_barrier(
            (terms[:, :half].astype(jnp.float32) + terms[:, half:].astype(jnp.float32)).astype(
                jnp.bfloat16
            )
        )
    return terms[:, 0].astype(jnp.float32)


def body(
    fwd_in, fwd_routes, router, bwd_in, bwd_routes, bwd_gates, w_gate, w_up, w_down, saved_pre
):
    width = fwd_in.shape[1]
    senders = lax.axis_size("expert")
    lanes = senders // EXPERTS
    inputs = shifted(fwd_in, "pipe", 1)
    cotan = shifted(bwd_in, "pipe", -1)
    wg = w_gate[0]
    wu = w_up[0]
    wd = w_down[0]
    fplaces = slot_places(fwd_routes)
    bplaces = slot_places(bwd_routes)
    xbuf = gather_rows(fplaces, inputs).reshape(EXPERTS, CAP, width)
    dbuf = gather_rows(bplaces, cotan).reshape(EXPERTS, CAP, width)
    logits = jnp.dot(inputs, router[0], preferred_element_type=jnp.float32)
    score = jax.nn.sigmoid(logits)
    chosen = jnp.take_along_axis(score, fwd_routes, axis=1)
    gates = chosen / jnp.sum(chosen, axis=1, keepdims=True)
    xsend = jnp.repeat(xbuf, lanes, axis=0)
    dsend = jnp.repeat(dbuf, lanes, axis=0)
    xrecv, drecv = (
        lax.all_to_all(xsend, "expert", split_axis=0, concat_axis=0, tiled=True),
        lax.all_to_all(dsend, "expert", split_axis=0, concat_axis=0, tiled=True),
    )
    rows = xrecv.reshape(senders * CAP, width)
    grads = drecv.reshape(senders * CAP, width)
    gpre = jnp.dot(rows, wg, preferred_element_type=jnp.float32)
    upre = jnp.dot(rows, wu, preferred_element_type=jnp.float32)
    hidden = (jax.nn.silu(gpre) * upre).astype(jnp.bfloat16)
    fpart = jnp.dot(hidden, wd, preferred_element_type=jnp.float32).astype(jnp.bfloat16)
    apre = saved_pre[0, 0].astype(jnp.float32)
    bpre = saved_pre[1, 0].astype(jnp.float32)
    dhid = lax.dot_general(grads, wd, (((1,), (1,)), ((), ())), preferred_element_type=jnp.float32)
    sig = jax.nn.sigmoid(apre)
    dgate = (dhid * bpre * sig * (1.0 + apre * (1.0 - sig))).astype(jnp.bfloat16)
    dup = (dhid * apre * sig).astype(jnp.bfloat16)
    bpart = lax.dot_general(dgate, wg, (((1,), (1,)), ((), ())), preferred_element_type=jnp.float32)
    bpart = (
        bpart
        + lax.dot_general(dup, wu, (((1,), (1,)), ((), ())), preferred_element_type=jnp.float32)
    ).astype(jnp.bfloat16)
    fback, bback = (
        lax.all_to_all(
            fpart.reshape(senders, CAP, width), "expert", split_axis=0, concat_axis=0, tiled=True
        ),
        lax.all_to_all(
            bpart.reshape(senders, CAP, width), "expert", split_axis=0, concat_axis=0, tiled=True
        ),
    )
    ysum = lane_tree(fback.reshape(EXPERTS, lanes, CAP, width)).reshape(EXPERTS * CAP, width)
    zsum = lane_tree(bback.reshape(EXPERTS, lanes, CAP, width)).reshape(EXPERTS * CAP, width)
    fwd_out = (inputs.astype(jnp.float32) + spread_back(fplaces, gates, ysum)).astype(jnp.bfloat16)
    bwd_out = (cotan.astype(jnp.float32) + spread_back(bplaces, bwd_gates, zsum)).astype(
        jnp.bfloat16
    )
    return (fwd_out, bwd_out)


def solution(mesh):
    in_specs = (
        P(("pipe", "expert"), None),
        P(("pipe", "expert"), None),
        P("pipe", None, None),
        P(("pipe", "expert"), None),
        P(("pipe", "expert"), None),
        P(("pipe", "expert"), None),
        P("pipe", None, "expert"),
        P("pipe", None, "expert"),
        P("pipe", "expert", None),
        P(None, "pipe", None, "expert"),
    )
    out_specs = (P(("pipe", "expert"), None), P(("pipe", "expert"), None))
    return jax.shard_map(body, mesh=mesh, in_specs=in_specs, out_specs=out_specs, check_vma=False)
```

profile of v0, /device:TPU:122, one launch (start us, length us, event | category | flops | bytes accessed | tf_op | source)
XLA Modules:
  0.0 1158.9 jit_solution(10122705491185196160)
XLA Ops:
  0.6 2.1 collective-permute-start
  2.7 0.8 copy.66
  3.7 0.2 reduce_window_sum.17
  3.9 0.2 select_reduce_fusion.3
  4.1 0.1 reshape.85
  4.3 0.7 multiply_add_fusion.1
  5.1 16.5 %collective-permute-done = bf16[64,3584]{1,0:T(8,128)(2,1)S(1)} collective-permute-done((bf16[64,3584]{1,0:T(8,128)(2,1)}, bf16[64,3584]{1,0:T(8,128)(2,1)S(1)}, u32[]{:S(2)}, u32[]{:S(2)}) %collective-permute-start) | collective-permute-done | bytes 458784 | tf_op jit(solution)/shard_map/ppermute | solution.py:13
  21.6 1.4 convolution_convert_fusion.2
  23.0 1.5 reshape.87
  24.5 4.2 broadcast_in_dim.46
  28.6 9.0 all-to-all-start
  37.7 1.9 collective-permute-start.1
  40.0 0.2 reduce_window_sum.18
  40.1 0.2 select_reduce_fusion.2
  40.6 29.2 %collective-permute-done.1 = bf16[64,3584]{1,0:T(8,128)(2,1)S(1)} collective-permute-done((bf16[64,3584]{1,0:T(8,128)(2,1)S(1)}, bf16[64,3584]{1,0:T(8,128)(2,1)S(1)}, u32[]{:S(2)}, u32[]{:S(2)}) %collective-permute-start.1) | collective-permute-done | bytes 458784 | tf_op jit(solution)/shard_map/ppermute | solution.py:13
  69.9 1.4 convolution_convert_fusion.1
  71.2 1.5 reshape.94
  72.7 234.9 %all-to-all-done = bf16[32,34,3584]{2,1,0:T(8,128)(2,1)} async-done(((bf16[32,34,3584]{2,1,0:T(8,128)(2,1)}), bf16[32,34,3584]{2,1,0:T(8,128)(2,1)}, u32[]{:S(2)}, u32[]{:S(2)}) %all-to-all-start) | async-done | bytes 7798816 | tf_op jit(solution)/shard_map/all_to_all | solution.py:76
  307.6 4.1 broadcast_in_dim.48
  311.8 20.0 %all-to-all-start.2 = ((bf16[32,34,3584]{2,1,0:T(8,128)(2,1)}), bf16[32,34,3584]{2,1,0:T(8,128)(2,1)}, u32[]{:S(2)}, u32[]{:S(2)}) async-start(bf16[32,34,3584]{2,1,0:T(8,128)(2,1)} %bitcast.60), calls=%async_computation.2 | async-start | bytes 18350080 | tf_op jit(solution)/shard_map/all_to_all | solution.py:77
  331.7 9.7 reshape.89
  341.4 6.5 fusion.13
  347.9 12.4 %convolution_convert_fusion = bf16[1088,3584]{1,0:T(8,128)(2,1)} fusion(bf16[1088,3584]{1,0:T(8,128)(2,1)} %reshape.89, bf16[1,128,3584]{2,1,0:T(8,128)(2,1)S(1)} %copy-done.2, bf16[1,3584,128]{2,1,0:T(8,128)(2,1)S(1)} %copy-done, f32[1088,128]{1,0:T(8,128)} %fusion.13), kind=kOutput, calls=%fused_computation.3 | convolution fusion | flops 2001223680 | bytes 17989632 | tf_op jit(solution)/shard_map/dot_general | solution.py:84
  360.3 9.6 reshape.90
  369.8 223.8 %all-to-all-done.2 = bf16[32,34,3584]{2,1,0:T(8,128)(2,1)} async-done(((bf16[32,34,3584]{2,1,0:T(8,128)(2,1)}), bf16[32,34,3584]{2,1,0:T(8,128)(2,1)}, u32[]{:S(2)}, u32[]{:S(2)}) %all-to-all-start.2) | async-done | bytes 7798816 | tf_op jit(solution)/shard_map/all_to_all | solution.py:77
  593.7 11.1 all-to-all-start.1
  604.8 9.7 reshape.96
  614.5 5.5 fusion.5
  620.0 7.7 fusion.11
  627.7 10.6 fusion
  638.3 9.7 reshape.97
  648.0 207.8 %all-to-all-done.1 = bf16[32,34,3584]{2,1,0:T(8,128)(2,1)} async-done(((bf16[32,34,3584]{2,1,0:T(8,128)(2,1)}), bf16[32,34,3584]{2,1,0:T(8,128)(2,1)}, u32[]{:S(2)}, u32[]{:S(2)}) %all-to-all-start.1) | async-done | bytes 7798816 | tf_op jit(solution)/shard_map/all_to_all | solution.py:97
  855.9 33.8 %all-to-all-start.3 = ((bf16[32,34,3584]{2,1,0:T(8,128)(2,1)}), bf16[32,34,3584]{2,1,0:T(8,128)(2,1)}, u32[]{:S(2)}, u32[]{:S(2)}) async-start(bf16[32,34,3584]{2,1,0:T(8,128)(2,1)} %reshape.97), calls=%async_computation.3 | async-start | bytes 18350080 | tf_op jit(solution)/shard_map/all_to_all | solution.py:100
  890.1 0.2 fusion.4
  890.3 1.5 gather_fusion
  892.3 4.3 fusion.50
  896.6 1.2 add_convert_fusion.1
  897.8 0.5 add_convert_fusion.3
  898.4 0.3 add_convert_fusion.5
  898.6 1.2 reshape.92
  899.9 246.3 %all-to-all-done.3 = bf16[32,34,3584]{2,1,0:T(8,128)(2,1)} async-done(((bf16[32,34,3584]{2,1,0:T(8,128)(2,1)}), bf16[32,34,3584]{2,1,0:T(8,128)(2,1)}, u32[]{:S(2)}, u32[]{:S(2)}) %all-to-all-start.3) | async-done | bytes 7798816 | tf_op jit(solution)/shard_map/all_to_all | solution.py:100
  1146.2 4.3 fusion.49
  1150.5 1.2 add_convert_fusion
  1151.8 0.5 add_convert_fusion.2
  1152.3 0.3 add_convert_fusion.4
  1152.6 1.2 reshape.99
  1153.8 2.5 add_convert_fusion.7
  1156.4 2.5 add_convert_fusion.6
  (40 shorter events, 1.8 us)
Async XLA Ops:
  0.6 347.3 %copy-start = (bf16[1,3584,128]{2,1,0:T(8,128)(2,1)S(1)}, bf16[1,3584,128]{2,1,0:T(8,128)(2,1)}, u32[]{:S(2)}) copy-start(bf16[1,3584,128]{2,1,0:T(8,128)(2,1)} %param.17) | copy-start | bytes 2752516
  0.6 20.9 %collective-permute-start = (bf16[64,3584]{1,0:T(8,128)(2,1)}, bf16[64,3584]{1,0:T(8,128)(2,1)S(1)}, u32[]{:S(2)}, u32[]{:S(2)}) collective-permute-start(bf16[64,3584]{1,0:T(8,128)(2,1)} %param.10), channel_id=1, source_target_pairs={{0,32},{32,64},{64,96},{96,128},{128,160},{160,192},{192,224},{224... | collective-permute-start | bytes 1376264 | tf_op jit(solution)/shard_map/ppermute | solution.py:13
  28.6 9.0 copy-start.9
  28.6 11.0 copy-start.7
  28.6 279.0 %all-to-all-start = ((bf16[32,34,3584]{2,1,0:T(8,128)(2,1)}), bf16[32,34,3584]{2,1,0:T(8,128)(2,1)}, u32[]{:S(2)}, u32[]{:S(2)}) async-start(bf16[32,34,3584]{2,1,0:T(8,128)(2,1)} %bitcast.59), calls=%async_computation | async-start | bytes 18350080 | tf_op jit(solution)/shard_map/all_to_all | solution.py:76
  37.7 32.2 %collective-permute-start.1 = (bf16[64,3584]{1,0:T(8,128)(2,1)S(1)}, bf16[64,3584]{1,0:T(8,128)(2,1)S(1)}, u32[]{:S(2)}, u32[]{:S(2)}) collective-permute-start(bf16[64,3584]{1,0:T(8,128)(2,1)S(1)} %copy-done.9), channel_id=1, source_target_pairs={{0,480},{32,0},{64,32},{96,64},{128,96},{160,128},{192,160},{224,1... | collective-permute-start | bytes 1376264 | tf_op jit(solution)/shard_map/ppermute | solution.py:13
  311.8 281.9 %all-to-all-start.2 = ((bf16[32,34,3584]{2,1,0:T(8,128)(2,1)}), bf16[32,34,3584]{2,1,0:T(8,128)(2,1)}, u32[]{:S(2)}, u32[]{:S(2)}) async-start(bf16[32,34,3584]{2,1,0:T(8,128)(2,1)} %bitcast.60), calls=%async_computation.2 | async-start | bytes 18350080 | tf_op jit(solution)/shard_map/all_to_all | solution.py:77
  341.4 6.5 copy-start.2
  593.7 262.2 %all-to-all-start.1 = ((bf16[32,34,3584]{2,1,0:T(8,128)(2,1)}), bf16[32,34,3584]{2,1,0:T(8,128)(2,1)}, u32[]{:S(2)}, u32[]{:S(2)}) async-start(bf16[32,34,3584]{2,1,0:T(8,128)(2,1)} %reshape.90), calls=%async_computation.1 | async-start | bytes 18350080 | tf_op jit(solution)/shard_map/all_to_all | solution.py:97
  614.5 5.5 copy-start.3
  614.5 5.5 copy-start.4
  648.0 241.7 %copy-start.6 = (s32[64,2]{0,1:T(2,128)S(1)}, s32[64,2]{0,1:T(2,128)}, u32[]{:S(2)}) copy-start(s32[64,2]{0,1:T(2,128)} %param.11) | copy-start | bytes 1540
  648.0 242.0 %copy-start.8 = (f32[64,2]{0,1:T(2,128)S(1)}, f32[64,2]{0,1:T(2,128)}, u32[]{:S(2)}) copy-start(f32[64,2]{0,1:T(2,128)} %param.15) | copy-start | bytes 1540
  648.0 242.1 %copy-start.5 = (bf16[1,3584,4]{1,2,0:T(4,128)(2,1)S(1)}, bf16[1,3584,4]{1,2,0:T(4,128)(2,1)}, u32[]{:S(2)}) copy-start(bf16[1,3584,4]{1,2,0:T(4,128)(2,1)} %param.12) | copy-start | bytes 86020
  855.9 290.3 %all-to-all-start.3 = ((bf16[32,34,3584]{2,1,0:T(8,128)(2,1)}), bf16[32,34,3584]{2,1,0:T(8,128)(2,1)}, u32[]{:S(2)}, u32[]{:S(2)}) async-start(bf16[32,34,3584]{2,1,0:T(8,128)(2,1)} %reshape.97), calls=%async_computation.3 | async-start | bytes 18350080 | tf_op jit(solution)/shard_map/all_to_all | solution.py:100
  1151.8 7.2 copy-start.1
where the time goes:
time: 1160 us
  waiting for transfers between devices  959 us (83%)
  starting transfers between devices  77.9 us (7%)
  local copies, waits for them, and re-layouts  64.5 us (6%)
  matrix products  50.7 us (4%)
    all_to_all x1, waiting for transfers between devices, body(): lax.all_to_all(bpart.reshape(senders, CAP, width), 'expert', split_axis=0...  246 us
    all_to_all x1, waiting for transfers between devices, body(): lax.all_to_all(xsend, 'expert', split_axis=0, concat_axis=0, tiled=True)  235 us
    all_to_all x1, waiting for transfers between devices, body(): lax.all_to_all(dsend, 'expert', split_axis=0, concat_axis=0, tiled=True)  224 us
    all_to_all x1, waiting for transfers between devices, body(): lax.all_to_all(fpart.reshape(senders, CAP, width), 'expert', split_axis=0...  208 us
    ppermute x2, waiting for transfers between devices, shifted(): lax.ppermute(array, axis, [(i, (i + by) % count) for i in range(count)])  45.7 us
    all_to_all x1, starting transfers between devices, body(): lax.all_to_all(bpart.reshape(senders, CAP, width), 'expert', split_axis=0...  33.8 us
  transfers between devices with their start and end apart: 6, of which 6 were waited for; matrix products, arithmetic and copies ran while one was open for 8% of the time, Pallas kernels for 0%

commit v1 on v0

v1 whole, which is shorter than its diff:
```python
import jax
import jax.numpy as jnp
from jax import lax
from jax.sharding import Mesh, PartitionSpec as P

EXPERTS = 4
TOP = 2
CAP = 34
LANES = 8
INFO = 128

AXES = ("x", "h", "c", "u", "v", "y")
SIZES = (4, 2, 2, 2, 2, 8)


def swap(array):
    return lax.ppermute(array, ("c", "u"), [(0, 0), (1, 2), (2, 1), (3, 3)])


def shift_and_swap(array, by):
    pairs = []
    for p in range(16):
        q = (p + by) % 16
        for u in range(2):
            source = p * 2 + u
            target = (q // 2) * 4 + u * 2 + q % 2
            pairs.append((source, target))
    return lax.ppermute(array, ("x", "h", "c", "u"), pairs)


def other_plane(array):
    return lax.ppermute(array, "v", [(0, 1), (1, 0)])


def other_core(array):
    return lax.ppermute(array, "c", [(0, 1), (1, 0)])


def experts_of_lane(block):
    own = swap(block)
    near = other_plane(own)
    return (own, near, other_core(own), other_core(near))


def saved_of_lane(saved, number):
    rows = saved.shape[1] // EXPERTS
    expert = lax.axis_index("u") * 2 + lax.axis_index("v")
    part = lax.dynamic_slice_in_dim(saved, (expert ^ number) * rows, rows, axis=1)
    pairs = []
    for c in range(2):
        for e in range(4):
            z = e ^ number
            pairs.append((c * 4 + e, (z // 2) * 4 + c * 2 + z % 2))
    return lax.ppermute(part, ("c", "u", "v"), pairs)


def slot_places(routes):
    rows = routes.shape[0]
    onehot = (routes[:, :, None] == jnp.arange(EXPERTS, dtype=jnp.int32)[None, None, :]).astype(
        jnp.int32
    )
    onehot = onehot.reshape(rows * TOP, EXPERTS)
    before = jnp.cumsum(onehot, axis=0) - onehot
    slot = jnp.sum(before * onehot, axis=1).reshape(rows, TOP)
    return routes * CAP + slot


def three_terms(values):
    high = lax.reduce_precision(values, 8, 7)
    middle = lax.reduce_precision(values - high, 8, 7)
    low = values - high - middle
    return [high, middle, low]


def body(
    fwd_in, fwd_routes, router, bwd_in, bwd_routes, bwd_gates, w_gate, w_up, w_down, saved_pre
):
    width = fwd_in.shape[1]
    tokens = fwd_in.shape[0]
    x = shift_and_swap(fwd_in, 1)
    q = shift_and_swap(bwd_in, -1)
    info = jnp.concatenate(
        [fwd_routes.astype(jnp.float32), slot_places(bwd_routes).astype(jnp.float32)]
        + three_terms(bwd_gates),
        axis=1,
    ).astype(jnp.bfloat16)
    info = swap(jnp.pad(info, ((0, 0), (0, INFO - info.shape[1]))))
    columns = swap(router[0].T)
    wgu = experts_of_lane(jnp.concatenate([w_gate[0], w_up[0]], axis=1))
    wd = experts_of_lane(w_down[0])
    saved = [saved_of_lane(saved_pre[:, 0], number) for number in range(EXPERTS)]

    gathered = lax.all_gather(jnp.concatenate([x, info], axis=1), "y", axis=0, tiled=True)
    grads = lax.all_gather(q, "y", axis=0, tiled=True)
    rows = gathered[:, :width]
    facts = gathered[:, width:].astype(jnp.float32)
    froutes = facts[:, 0:2].astype(jnp.int32)
    bplaces = facts[:, 2:4].astype(jnp.int32)
    bgates = facts[:, 4:6] + facts[:, 6:8] + facts[:, 8:10]
    broutes = bplaces // CAP
    e0 = lax.axis_index("c") * 2 + lax.axis_index("v")

    score = jax.nn.sigmoid(
        lax.dot_general(rows, columns, (((1,), (1,)), ((), ())), preferred_element_type=jnp.float32)
    )
    chosen = jnp.take_along_axis(score, froutes, axis=1)
    fgates = chosen / jnp.sum(chosen, axis=1, keepdims=True)

    source = jnp.arange(rows.shape[0], dtype=jnp.int32)[:, None] // tokens
    hidden = []
    for number in range(EXPERTS):
        named = froutes == (e0 ^ number)
        weight = jnp.sum(jnp.where(named, fgates, 0.0), axis=1, keepdims=True)
        pre = jnp.dot(rows, wgu[number], preferred_element_type=jnp.float32)
        half = pre.shape[1] // 2
        hidden.append((jax.nn.silu(pre[:, :half]) * pre[:, half:] * weight).astype(jnp.bfloat16))
    fpart = jnp.dot(
        jnp.concatenate(hidden, axis=1),
        jnp.concatenate(wd, axis=0),
        preferred_element_type=jnp.float32,
    ).astype(jnp.bfloat16)
    fsum = lax.psum_scatter(fpart, "y", scatter_dimension=0, tiled=True)

    dpre = []
    for number in range(EXPERTS):
        named = broutes == (e0 ^ number)
        weight = jnp.sum(jnp.where(named, bgates, 0.0), axis=1, keepdims=True)
        slot = source * CAP + bplaces - broutes * CAP + 1
        spot = jnp.sum(jnp.where(named, slot, 0), axis=1, keepdims=True) - 1
        pick = (spot == jnp.arange(LANES * CAP, dtype=jnp.int32)[None, :]).astype(jnp.bfloat16)
        apre = jnp.dot(pick, saved[number][0], preferred_element_type=jnp.float32)
        bpre = jnp.dot(pick, saved[number][1], preferred_element_type=jnp.float32)
        dhid = lax.dot_general(
            grads, wd[number], (((1,), (1,)), ((), ())), preferred_element_type=jnp.float32
        )
        sig = jax.nn.sigmoid(apre)
        dhid = dhid * weight
        dpre.append((dhid * bpre * sig * (1.0 + apre * (1.0 - sig))).astype(jnp.bfloat16))
        dpre.append((dhid * apre * sig).astype(jnp.bfloat16))
    bpart = lax.dot_general(
        jnp.concatenate(dpre, axis=1),
        jnp.concatenate(wgu, axis=1),
        (((1,), (1,)), ((), ())),
        preferred_element_type=jnp.float32,
    ).astype(jnp.bfloat16)
    bsum = lax.psum_scatter(bpart, "y", scatter_dimension=0, tiled=True)

    fwd_out = (x.astype(jnp.float32) + fsum.astype(jnp.float32)).astype(jnp.bfloat16)
    bwd_out = (q.astype(jnp.float32) + bsum.astype(jnp.float32)).astype(jnp.bfloat16)
    return (swap(fwd_out), swap(bwd_out))


def solution(mesh):
    fine = Mesh(mesh.devices.reshape(SIZES), AXES)
    section = ("x", "h", "c")
    part = ("u", "v", "y")
    both = P(AXES, None)
    in_specs = (
        both,
        both,
        P(section, None, None),
        both,
        both,
        both,
        P(section, None, part),
        P(section, None, part),
        P(section, part, None),
        P(None, section, None, part),
    )
    return jax.shard_map(
        body, mesh=fine, in_specs=in_specs, out_specs=(both, both), check_vma=False
    )
```

time: 1160 us -> 348 us (0.30)
  the two profiles are of different devices: /device:TPU:122 before, /device:TPU:1 now
where the time goes in v1:
time: 348 us; the launch traced here: 347 us
  waiting for transfers between devices  172 us (49%)
  starting transfers between devices  85.6 us (25%)
  matrix products  46.6 us (13%)
  local copies, waits for them, and re-layouts  16.4 us (5%)
  between operations  14.4 us (4%)
  other arithmetic  11.6 us (3%)
    reduce_scatter x1, waiting for transfers between devices, body(): fsum = lax.psum_scatter(fpart, 'y', scatter_dimension=0, tiled=True)  48.9 us
    ppermute x6, waiting for transfers between devices, swap(): return lax.ppermute(array, ('c', 'u'), [(0, 0), (1, 2), (2, 1), (3, 3)])  35.2 us
    ppermute x2, waiting for transfers between devices, other_plane(): return lax.ppermute(array, 'v', [(0, 1), (1, 0)])  34.8 us
    reduce_scatter x1, waiting for transfers between devices, body(): bsum = lax.psum_scatter(bpart, 'y', scatter_dimension=0, tiled=True)  33.5 us
    ppermute x4, starting transfers between devices, saved_of_lane(): return lax.ppermute(part, ('c', 'u', 'v'), pairs)  28.5 us
    ppermute x2, starting transfers between devices, shift_and_swap(): return lax.ppermute(array, ('x', 'h', 'c', 'u'), pairs)  22.7 us
    ppermute x6, starting transfers between devices, swap(): return lax.ppermute(array, ('c', 'u'), [(0, 0), (1, 2), (2, 1), (3, 3)])  20.3 us
    dot_general x4, matrix products, body(): lax.dot_general(grads, wd[number], (((1,), (1,)), ((), ())), preferred_el...  11.1 us
  transfers between devices with their start and end apart: 22, of which 11 were waited for; matrix products, arithmetic and copies ran while one was open for 18% of the time, Pallas kernels for 0%

profile of v1, /device:TPU:1, one launch (start us, length us, event | category | flops | bytes accessed | tf_op | source)
XLA Modules:
  0.0 346.6 jit_solution(8396658015003041866)
XLA Ops:
  7.2 12.0 %collective-permute-start = (bf16[64,3584]{1,0:T(8,128)(2,1)}, bf16[64,3584]{1,0:T(8,128)(2,1)S(1)}, u32[]{:S(2)}, u32[]{:S(2)}) collective-permute-start(bf16[64,3584]{1,0:T(8,128)(2,1)} %param.10), channel_id=1, source_target_pairs={{0,16},{16,48},{32,64},{48,96},{64,80},{80,112},{96,128},{112,160}... | collective-permute-start | bytes 1376264 | tf_op jit(solution)/shard_map/ppermute | solution.py:28
  22.4 1.9 collective-permute-start.1
  24.3 4.3 %collective-permute-done.1 = bf16[64,128]{1,0:T(8,128)(2,1)S(1)} collective-permute-done((bf16[64,128]{1,0:T(8,128)(2,1)S(1)}, bf16[64,128]{1,0:T(8,128)(2,1)S(1)}, u32[]{:S(2)}, u32[]{:S(2)}) %collective-permute-start.1) | collective-permute-done | bytes 16416 | tf_op jit(solution)/shard_map/ppermute | solution.py:17
  28.6 2.0 collective-permute-done
  31.5 10.6 %collective-permute-start.12 = (bf16[64,3584]{1,0:T(8,128)(2,1)}, bf16[64,3584]{1,0:T(8,128)(2,1)S(1)}, u32[]{:S(2)}, u32[]{:S(2)}) collective-permute-start(bf16[64,3584]{1,0:T(8,128)(2,1)} %param.13), channel_id=1, source_target_pairs={{0,464},{16,496},{32,0},{48,32},{64,16},{80,48},{96,64},{112,96},{... | collective-permute-start | bytes 1376264 | tf_op jit(solution)/shard_map/ppermute | solution.py:28
  42.1 1.6 collective-permute-done.12
  44.6 2.2 collective-permute-start.3
  46.8 1.9 dynamic-slice_bitcast_fusion
  48.7 12.3 %collective-permute-start.16 = (bf16[2,272,128]{2,1,0:T(8,128)(2,1)}, bf16[2,272,128]{2,1,0:T(8,128)(2,1)}, u32[]{:S(2)}, u32[]{:S(2)}) collective-permute-start(bf16[2,272,128]{2,1,0:T(8,128)(2,1)} %get-tuple-element.20), channel_id=1, source_target_pairs={{0,40},{8,32},{16,8},{24,0},{32,56},{40,48},{48,24},{56,16},{1,41}... | collective-permute-start | bytes 417800 | tf_op jit(solution)/shard_map/ppermute | solution.py:54
  61.0 9.4 %collective-permute-start.14 = (bf16[2,272,128]{2,1,0:T(8,128)(2,1)}, bf16[2,272,128]{2,1,0:T(8,128)(2,1)}, u32[]{:S(2)}, u32[]{:S(2)}) collective-permute-start(bf16[2,272,128]{2,1,0:T(8,128)(2,1)} %get-tuple-element.21), channel_id=1, source_target_pairs={{0,8},{8,0},{16,40},{24,32},{32,24},{40,16},{48,56},{56,48},{1,9},... | collective-permute-start | bytes 417800 | tf_op jit(solution)/shard_map/ppermute | solution.py:54
  70.4 1.9 collective-permute-start.7
  72.4 1.7 pad_maximum_fusion
  74.0 4.5 %collective-permute-start.2 = (bf16[3584,256]{1,0:T(8,128)(2,1)S(1)}, bf16[3584,256]{1,0:T(8,128)(2,1)}, u32[]{:S(2)}, u32[]{:S(2)}) collective-permute-start(bf16[3584,256]{1,0:T(8,128)(2,1)S(1)} %pad_maximum_fusion), channel_id=1, source_target_pairs={{0,0},{16,32},{32,16},{48,48},{1,1},{17,33},{33,17},{49,49},{2,2},... | collective-permute-start | bytes 5505032 | tf_op jit(solution)/shard_map/ppermute | solution.py:17
  78.6 9.5 %all-gather.3.cloned.1.call-done = bf16[512,3712]{1,0:T(8,128)(2,1)} async-done(((bf16[64,3712]{1,0:T(8,128)(2,1)}), bf16[512,3712]{1,0:T(8,128)(2,1)}) %all-gather.3.cloned.1.call-update) | async-done | bytes 3801104 | tf_op jit(solution)/shard_map/all_gather | solution.py:93
  90.4 4.9 %collective-permute-start.13 = (bf16[2,272,128]{2,1,0:T(8,128)(2,1)S(1)}, bf16[2,272,128]{2,1,0:T(8,128)(2,1)}, u32[]{:S(2)}, u32[]{:S(2)}) collective-permute-start(bf16[2,272,128]{2,1,0:T(8,128)(2,1)S(1)} %get-tuple-element.22), channel_id=1, source_target_pairs={{0,0},{8,8},{16,32},{24,40},{32,16},{40,24},{48,48},{56,56},{1,1},... | collective-permute-start | bytes 417800 | tf_op jit(solution)/shard_map/ppermute | solution.py:54
  95.3 19.8 %collective-permute-done.7 = bf16[128,3584]{1,0:T(8,128)(2,1)} collective-permute-done((bf16[128,3584]{1,0:T(8,128)(2,1)}, bf16[128,3584]{1,0:T(8,128)(2,1)}, u32[]{:S(2)}, u32[]{:S(2)}) %collective-permute-start.7) | collective-permute-done | bytes 917536 | tf_op jit(solution)/shard_map/ppermute | solution.py:17
  115.1 1.9 collective-permute-start.8
  117.0 3.1 fusion.53
  120.3 9.1 %gather_fusion = f32[1024]{0:T(1024)S(1)} fusion(f32[512,4]{0,1:T(4,128)S(1)} %fusion.53, s32[1024]{0:T(1024)S(1)} %reshape.90), kind=kCustom, calls=%fused_computation | custom fusion | bytes 16384 | tf_op jit(solution)/shard_map/jit(take_along_axis)/gather | solution.py:106
  129.8 6.5 %collective-permute-done.13 = bf16[2,272,128]{2,1,0:T(8,128)(2,1)} collective-permute-done((bf16[2,272,128]{2,1,0:T(8,128)(2,1)S(1)}, bf16[2,272,128]{2,1,0:T(8,128)(2,1)}, u32[]{:S(2)}, u32[]{:S(2)}) %collective-permute-start.13) | collective-permute-done | bytes 139296 | tf_op jit(solution)/shard_map/ppermute | solution.py:54
  136.2 1.9 collective-permute-start.15
  138.1 1.3 fusion.59
  139.8 2.4 collective-permute-start.9
  142.2 7.3 %collective-permute-done.8 = bf16[128,3584]{1,0:T(8,128)(2,1)} collective-permute-done((bf16[128,3584]{1,0:T(8,128)(2,1)}, bf16[128,3584]{1,0:T(8,128)(2,1)}, u32[]{:S(2)}, u32[]{:S(2)}) %collective-permute-start.8) | collective-permute-done | bytes 917536 | tf_op jit(solution)/shard_map/ppermute | solution.py:32
  149.5 1.9 collective-permute-start.10
  151.4 1.9 collective-permute-start.4
  155.8 3.7 %convolution_multiply_fusion.7 = f32[512,128]{0,1:T(8,128)S(1)} fusion(bf16[512,3584]{1,0:T(8,128)(2,1)} %all-gather.5.cloned.1.call-done, bf16[128,3584]{1,0:T(8,128)(2,1)} %collective-permute-done.7, f32[512]{0:T(512)S(1)} %get-tuple-element.13), kind=kOutput, calls=%fused_computation.44 | convolution fusion | flops 469827584 | bytes 4851712 | tf_op jit(solution)/shard_map/dot_general | solution.py:133
  159.6 1.3 fusion.37
  161.0 2.5 convolution_multiply_fusion.5
  163.4 1.3 fusion.39
  164.7 2.4 collective-permute-start.5
  167.2 27.5 %collective-permute-done.4 = bf16[3584,256]{1,0:T(8,128)(2,1)} collective-permute-done((bf16[3584,256]{1,0:T(8,128)(2,1)}, bf16[3584,256]{1,0:T(8,128)(2,1)}, u32[]{:S(2)}, u32[]{:S(2)}) %collective-permute-start.4) | collective-permute-done | bytes 1835040 | tf_op jit(solution)/shard_map/ppermute | solution.py:32
  194.7 3.4 collective-permute-start.6
  198.1 1.3 fusion.57
  199.5 1.3 fusion.56
  200.8 2.5 convolution_multiply_fusion.3
  203.2 1.3 fusion.41
  204.6 2.5 convolution_multiply_fusion.1
  207.1 1.3 fusion.43
  209.8 7.0 %fusion.8 = bf16[512,3584]{1,0:T(8,128)(2,1)} fusion(bf16[512,1024]{0,1:T(8,128)(2,1)S(1)} %fusion.87, bf16[3584,256]{1,0:T(8,128)(2,1)S(1)} %collective-permute-done.6, bf16[3584,256]{1,0:T(8,128)(2,1)S(1)} %collective-permute-done.5, bf16[3584,256]{1,0:T(8,128)(2,1)} %collective-permute-done.4, bf16[3584,256]{1,0:T(8,128)(2,1)} %collective-permute-done.2), kind=kOutput, calls=%fused_computation.9 | convolution fusion | flops 3789291520 | bytes 12058624 | tf_op jit(solution)/shard_map/dot_general | solution.py:140
  217.2 3.9 %fusion.26 = f32[512,256]{0,1:T(8,128)S(1)} fusion(bf16[3584,256]{1,0:T(8,128)(2,1)} %collective-permute-done.2, bf16[512,3712]{1,0:T(8,128)(2,1)} %all-gather.3.cloned.1.call-done), kind=kOutput, calls=%fused_computation.26 | convolution fusion | flops 939524096 | bytes 6029312 | tf_op jit(solution)/shard_map/dot_general | solution.py:114
  222.8 2.7 fusion.22
  226.8 6.2 %convolution_convert_fusion = bf16[512,3584]{1,0:T(8,128)(2,1)} fusion(bf16[128,3584]{1,0:T(8,128)(2,1)} %collective-permute-done.10, bf16[128,3584]{1,0:T(8,128)(2,1)} %collective-permute-done.9, bf16[128,3584]{1,0:T(8,128)(2,1)} %collective-permute-done.8, bf16[128,3584]{1,0:T(8,128)(2,1)} %collective-permute-done.7, bf16[512,128]{0,1:T(8,128)(2,1)S(1)} %fusion.76, ...), kind=kOutput, calls=%fused_computation.10 | convolution fusion | flops 1897660416 | bytes 7864320 | tf_op jit(solution)/shard_map/dot_general | solution.py:117
  233.1 33.5 %reduce-scatter.5.cloned.1.call-done = bf16[64,3584]{1,0:T(8,128)(2,1)} async-done(((bf16[512,3584]{1,0:T(8,128)(2,1)}), bf16[64,3584]{1,0:T(8,128)(2,1)}) %reduce-scatter.5.cloned.1.call-update) | async-done | bytes 458768 | tf_op jit(solution)/shard_map/reduce_scatter | solution.py:146
  267.7 4.9 %collective-permute-start.17 = (bf16[64,3584]{1,0:T(8,128)(2,1)S(1)}, bf16[64,3584]{1,0:T(8,128)(2,1)S(1)}, u32[]{:S(2)}, u32[]{:S(2)}) collective-permute-start(bf16[64,3584]{1,0:T(8,128)(2,1)S(1)} %add_convert_fusion), channel_id=1, source_target_pairs={{0,0},{16,32},{32,16},{48,48},{1,1},{17,33},{33,17},{49,49},{2,2},... | collective-permute-start | bytes 1376264 | tf_op jit(solution)/shard_map/ppermute | solution.py:17
  272.6 48.9 %reduce-scatter.3.cloned.1.call-done = bf16[64,3584]{1,0:T(8,128)(2,1)} async-done(((bf16[512,3584]{1,0:T(8,128)(2,1)}), bf16[64,3584]{1,0:T(8,128)(2,1)}) %reduce-scatter.3.cloned.1.call-update) | async-done | bytes 458768 | tf_op jit(solution)/shard_map/reduce_scatter | solution.py:122
  322.6 4.9 %collective-permute-start.11 = (bf16[64,3584]{1,0:T(8,128)(2,1)S(1)}, bf16[64,3584]{1,0:T(8,128)(2,1)S(1)}, u32[]{:S(2)}, u32[]{:S(2)}) collective-permute-start(bf16[64,3584]{1,0:T(8,128)(2,1)S(1)} %add_convert_fusion.1), channel_id=1, source_target_pairs={{0,0},{16,32},{32,16},{48,48},{1,1},{17,33},{33,17},{49,49},{2,2},... | collective-permute-start | bytes 1376264 | tf_op jit(solution)/shard_map/ppermute | solution.py:17
  327.5 11.1 %collective-permute-done.11 = bf16[64,3584]{1,0:T(8,128)(2,1)S(1)} collective-permute-done((bf16[64,3584]{1,0:T(8,128)(2,1)S(1)}, bf16[64,3584]{1,0:T(8,128)(2,1)S(1)}, u32[]{:S(2)}, u32[]{:S(2)}) %collective-permute-start.11) | collective-permute-done | bytes 458784 | tf_op jit(solution)/shard_map/ppermute | solution.py:17
  (74 shorter events, 19.2 us)
Async XLA Ops:
  7.2 80.9 %all-gather.3.cloned.1.call-start = ((), (), s32[]{:S(2)}) async-start(), calls=%async_computation.2 | async-start | bytes 4276224 | tf_op jit(solution)/shard_map/all_gather | solution.py:93
  7.2 23.4 %collective-permute-start = (bf16[64,3584]{1,0:T(8,128)(2,1)}, bf16[64,3584]{1,0:T(8,128)(2,1)S(1)}, u32[]{:S(2)}, u32[]{:S(2)}) collective-permute-start(bf16[64,3584]{1,0:T(8,128)(2,1)} %param.10), channel_id=1, source_target_pairs={{0,16},{16,48},{32,64},{48,96},{64,80},{80,112},{96,128},{112,160}... | collective-permute-start | bytes 1376264 | tf_op jit(solution)/shard_map/ppermute | solution.py:28
  22.4 6.2 %collective-permute-start.1 = (bf16[64,128]{1,0:T(8,128)(2,1)S(1)}, bf16[64,128]{1,0:T(8,128)(2,1)S(1)}, u32[]{:S(2)}, u32[]{:S(2)}) collective-permute-start(bf16[64,128]{1,0:T(8,128)(2,1)S(1)} %pad.4), channel_id=1, source_target_pairs={{0,0},{16,32},{32,16},{48,48},{1,1},{17,33},{33,17},{49,49},{2,2},... | collective-permute-start | bytes 49160 | tf_op jit(solution)/shard_map/ppermute | solution.py:17
  31.4 124.4 %all-gather.5.cloned.1.call-start = ((), (), s32[]{:S(2)}) async-start(), calls=%async_computation.4 | async-start | bytes 4128768 | tf_op jit(solution)/shard_map/all_gather | solution.py:94
  31.5 12.3 %collective-permute-start.12 = (bf16[64,3584]{1,0:T(8,128)(2,1)}, bf16[64,3584]{1,0:T(8,128)(2,1)S(1)}, u32[]{:S(2)}, u32[]{:S(2)}) collective-permute-start(bf16[64,3584]{1,0:T(8,128)(2,1)} %param.13), channel_id=1, source_target_pairs={{0,464},{16,496},{32,0},{48,32},{64,16},{80,48},{96,64},{112,96},{... | collective-permute-start | bytes 1376264 | tf_op jit(solution)/shard_map/ppermute | solution.py:28
  43.8 0.8 copy-start.1
  44.6 222.0 %reduce-scatter.5.cloned.1.call-start = ((), (), s32[]{:S(2)}) async-start(), calls=%async_computation.5 | async-start | bytes 4128768 | tf_op jit(solution)/shard_map/reduce_scatter | solution.py:146
  44.6 45.7 %collective-permute-start.3 = (bf16[4,3584]{1,0:T(4,128)(2,1)}, bf16[4,3584]{1,0:T(4,128)(2,1)S(1)}, u32[]{:S(2)}, u32[]{:S(2)}) collective-permute-start(bf16[4,3584]{1,0:T(4,128)(2,1)} %bitcast.59), channel_id=1, source_target_pairs={{0,0},{16,32},{32,16},{48,48},{1,1},{17,33},{33,17},{49,49},{2,2},... | collective-permute-start | bytes 86024 | tf_op jit(solution)/shard_map/ppermute | solution.py:17
  48.7 150.8 %collective-permute-start.16 = (bf16[2,272,128]{2,1,0:T(8,128)(2,1)}, bf16[2,272,128]{2,1,0:T(8,128)(2,1)}, u32[]{:S(2)}, u32[]{:S(2)}) collective-permute-start(bf16[2,272,128]{2,1,0:T(8,128)(2,1)} %get-tuple-element.20), channel_id=1, source_target_pairs={{0,40},{8,32},{16,8},{24,0},{32,56},{40,48},{48,24},{56,16},{1,41}... | collective-permute-start | bytes 417800 | tf_op jit(solution)/shard_map/ppermute | solution.py:54
  61.0 78.7 %collective-permute-start.14 = (bf16[2,272,128]{2,1,0:T(8,128)(2,1)}, bf16[2,272,128]{2,1,0:T(8,128)(2,1)}, u32[]{:S(2)}, u32[]{:S(2)}) collective-permute-start(bf16[2,272,128]{2,1,0:T(8,128)(2,1)} %get-tuple-element.21), channel_id=1, source_target_pairs={{0,8},{8,0},{16,40},{24,32},{32,24},{40,16},{48,56},{56,48},{1,9},... | collective-permute-start | bytes 417800 | tf_op jit(solution)/shard_map/ppermute | solution.py:54
  70.4 44.6 %collective-permute-start.7 = (bf16[128,3584]{1,0:T(8,128)(2,1)}, bf16[128,3584]{1,0:T(8,128)(2,1)}, u32[]{:S(2)}, u32[]{:S(2)}) collective-permute-start(bf16[128,3584]{1,0:T(8,128)(2,1)} %bitcast.58), channel_id=1, source_target_pairs={{0,0},{16,32},{32,16},{48,48},{1,1},{17,33},{33,17},{49,49},{2,2},... | collective-permute-start | bytes 2752520 | tf_op jit(solution)/shard_map/ppermute | solution.py:17
  74.0 77.4 %collective-permute-start.2 = (bf16[3584,256]{1,0:T(8,128)(2,1)S(1)}, bf16[3584,256]{1,0:T(8,128)(2,1)}, u32[]{:S(2)}, u32[]{:S(2)}) collective-permute-start(bf16[3584,256]{1,0:T(8,128)(2,1)S(1)} %pad_maximum_fusion), channel_id=1, source_target_pairs={{0,0},{16,32},{32,16},{48,48},{1,1},{17,33},{33,17},{49,49},{2,2},... | collective-permute-start | bytes 5505032 | tf_op jit(solution)/shard_map/ppermute | solution.py:17
  90.4 45.9 %collective-permute-start.13 = (bf16[2,272,128]{2,1,0:T(8,128)(2,1)S(1)}, bf16[2,272,128]{2,1,0:T(8,128)(2,1)}, u32[]{:S(2)}, u32[]{:S(2)}) collective-permute-start(bf16[2,272,128]{2,1,0:T(8,128)(2,1)S(1)} %get-tuple-element.22), channel_id=1, source_target_pairs={{0,0},{8,8},{16,32},{24,40},{32,16},{40,24},{48,48},{56,56},{1,1},... | collective-permute-start | bytes 417800 | tf_op jit(solution)/shard_map/ppermute | solution.py:54
  115.1 34.4 %collective-permute-start.8 = (bf16[128,3584]{1,0:T(8,128)(2,1)}, bf16[128,3584]{1,0:T(8,128)(2,1)}, u32[]{:S(2)}, u32[]{:S(2)}) collective-permute-start(bf16[128,3584]{1,0:T(8,128)(2,1)} %collective-permute-done.7), channel_id=1, source_target_pairs={{0,8},{8,0},{1,9},{9,1},{2,10},{10,2},{3,11},{11,3},{4,12},{12,4},... | collective-permute-start | bytes 2752520 | tf_op jit(solution)/shard_map/ppermute | solution.py:32
  136.2 28.5 %collective-permute-start.15 = (bf16[2,272,128]{2,1,0:T(8,128)(2,1)}, bf16[2,272,128]{2,1,0:T(8,128)(2,1)}, u32[]{:S(2)}, u32[]{:S(2)}) collective-permute-start(bf16[2,272,128]{2,1,0:T(8,128)(2,1)} %get-tuple-element.23), channel_id=1, source_target_pairs={{0,32},{8,40},{16,0},{24,8},{32,48},{40,56},{48,16},{56,24},{1,33}... | collective-permute-start | bytes 417800 | tf_op jit(solution)/shard_map/ppermute | solution.py:54
  139.8 61.0 %collective-permute-start.9 = (bf16[128,3584]{1,0:T(8,128)(2,1)}, bf16[128,3584]{1,0:T(8,128)(2,1)}, u32[]{:S(2)}, u32[]{:S(2)}) collective-permute-start(bf16[128,3584]{1,0:T(8,128)(2,1)} %collective-permute-done.7), channel_id=1, source_target_pairs={{0,32},{32,0},{1,33},{33,1},{2,34},{34,2},{3,35},{35,3},{4,36},{36... | collective-permute-start | bytes 2752520 | tf_op jit(solution)/shard_map/ppermute | solution.py:36
  149.5 55.2 %collective-permute-start.10 = (bf16[128,3584]{1,0:T(8,128)(2,1)}, bf16[128,3584]{1,0:T(8,128)(2,1)}, u32[]{:S(2)}, u32[]{:S(2)}) collective-permute-start(bf16[128,3584]{1,0:T(8,128)(2,1)} %collective-permute-done.8), channel_id=1, source_target_pairs={{0,32},{32,0},{1,33},{33,1},{2,34},{34,2},{3,35},{35,3},{4,36},{36... | collective-permute-start | bytes 2752520 | tf_op jit(solution)/shard_map/ppermute | solution.py:36
  151.4 43.3 %collective-permute-start.4 = (bf16[3584,256]{1,0:T(8,128)(2,1)}, bf16[3584,256]{1,0:T(8,128)(2,1)}, u32[]{:S(2)}, u32[]{:S(2)}) collective-permute-start(bf16[3584,256]{1,0:T(8,128)(2,1)} %collective-permute-done.2), channel_id=1, source_target_pairs={{0,8},{8,0},{1,9},{9,1},{2,10},{10,2},{3,11},{11,3},{4,12},{12,4},... | collective-permute-start | bytes 5505032 | tf_op jit(solution)/shard_map/ppermute | solution.py:32
  155.8 5.1 %copy-start = (bf16[512,3584]{1,0:T(8,128)(2,1)S(1)}, bf16[512,3584]{1,0:T(8,128)(2,1)}, u32[]{:S(2)}) copy-start(bf16[512,3584]{1,0:T(8,128)(2,1)} %all-gather.5.cloned.1.call-done) | copy-start | bytes 11010052
  164.7 43.8 %collective-permute-start.5 = (bf16[3584,256]{1,0:T(8,128)(2,1)}, bf16[3584,256]{1,0:T(8,128)(2,1)S(1)}, u32[]{:S(2)}, u32[]{:S(2)}) collective-permute-start(bf16[3584,256]{1,0:T(8,128)(2,1)} %collective-permute-done.2), channel_id=1, source_target_pairs={{0,32},{32,0},{1,33},{33,1},{2,34},{34,2},{3,35},{35,3},{4,36},{36... | collective-permute-start | bytes 5505032 | tf_op jit(solution)/shard_map/ppermute | solution.py:36
  194.7 13.9 %collective-permute-start.6 = (bf16[3584,256]{1,0:T(8,128)(2,1)}, bf16[3584,256]{1,0:T(8,128)(2,1)S(1)}, u32[]{:S(2)}, u32[]{:S(2)}) collective-permute-start(bf16[3584,256]{1,0:T(8,128)(2,1)} %collective-permute-done.4), channel_id=1, source_target_pairs={{0,32},{32,0},{1,33},{33,1},{2,34},{34,2},{3,35},{35,3},{4,36},{36... | collective-permute-start | bytes 5505032 | tf_op jit(solution)/shard_map/ppermute | solution.py:36
  208.5 1.3 copy-start.4
  216.8 104.7 %reduce-scatter.3.cloned.1.call-start = ((), (), s32[]{:S(2)}) async-start(), calls=%async_computation.3 | async-start | bytes 4128768 | tf_op jit(solution)/shard_map/reduce_scatter | solution.py:122
  217.2 4.0 %copy-start.3 = (bf16[512,3712]{1,0:T(8,128)(2,1)S(1)}, bf16[512,3712]{1,0:T(8,128)(2,1)}, u32[]{:S(2)}) copy-start(bf16[512,3712]{1,0:T(8,128)(2,1)} %all-gather.3.cloned.1.call-done) | copy-start | bytes 11403268
  217.2 4.3 %copy-start.5 = (bf16[3584,256]{1,0:T(8,128)(2,1)S(1)}, bf16[3584,256]{1,0:T(8,128)(2,1)}, u32[]{:S(2)}) copy-start(bf16[3584,256]{1,0:T(8,128)(2,1)} %copy-done.4) | copy-start | bytes 5505028
  233.0 33.5 %copy-start.2 = (bf16[64,3584]{1,0:T(8,128)(2,1)S(1)}, bf16[64,3584]{1,0:T(8,128)(2,1)}, u32[]{:S(2)}) copy-start(bf16[64,3584]{1,0:T(8,128)(2,1)} %copy-done.1) | copy-start | bytes 1376260
  267.7 59.8 %collective-permute-start.17 = (bf16[64,3584]{1,0:T(8,128)(2,1)S(1)}, bf16[64,3584]{1,0:T(8,128)(2,1)S(1)}, u32[]{:S(2)}, u32[]{:S(2)}) collective-permute-start(bf16[64,3584]{1,0:T(8,128)(2,1)S(1)} %add_convert_fusion), channel_id=1, source_target_pairs={{0,0},{16,32},{32,16},{48,48},{1,1},{17,33},{33,17},{49,49},{2,2},... | collective-permute-start | bytes 1376264 | tf_op jit(solution)/shard_map/ppermute | solution.py:17
  322.6 15.9 %collective-permute-start.11 = (bf16[64,3584]{1,0:T(8,128)(2,1)S(1)}, bf16[64,3584]{1,0:T(8,128)(2,1)S(1)}, u32[]{:S(2)}, u32[]{:S(2)}) collective-permute-start(bf16[64,3584]{1,0:T(8,128)(2,1)S(1)} %add_convert_fusion.1), channel_id=1, source_target_pairs={{0,0},{16,32},{32,16},{48,48},{1,1},{17,33},{33,17},{49,49},{2,2},... | collective-permute-start | bytes 1376264 | tf_op jit(solution)/shard_map/ppermute | solution.py:17
Sparse Core Ops, SparseCore 0:
  31.6 56.4 all-gather.2
  90.7 51.2 all-gather.4
  216.9 49.5 reduce-scatter.4
  269.3 52.1 reduce-scatter.2

commit v2 on v1

v2 whole, which is shorter than its diff:
```python
import jax
import jax.numpy as jnp
from jax import lax
from jax.experimental import pallas as pl
from jax.experimental.pallas import tpu as pltpu
from jax.sharding import Mesh, PartitionSpec as P

EXPERTS = 4
TOP = 2
CAP = 34
LANES = 8
INFO = 128
VMEM = 32 << 20

AXES = ("x", "h", "c", "u", "v", "y")
SIZES = (4, 2, 2, 2, 2, 8)


def swap(array):
    return lax.ppermute(array, ("c", "u"), [(0, 0), (1, 2), (2, 1), (3, 3)])


def shift_and_swap(array, by):
    pairs = []
    for p in range(16):
        q = (p + by) % 16
        for u in range(2):
            source = p * 2 + u
            target = (q // 2) * 4 + u * 2 + q % 2
            pairs.append((source, target))
    return lax.ppermute(array, ("x", "h", "c", "u"), pairs)


def other_plane(array):
    return lax.ppermute(array, "v", [(0, 1), (1, 0)])


def other_core(array):
    return lax.ppermute(array, "c", [(0, 1), (1, 0)])


def saved_of_lane(saved, number):
    rows = saved.shape[1] // EXPERTS
    expert = lax.axis_index("u") * 2 + lax.axis_index("v")
    part = lax.dynamic_slice_in_dim(saved, (expert ^ number) * rows, rows, axis=1)
    pairs = []
    for c in range(2):
        for e in range(4):
            z = e ^ number
            pairs.append((c * 4 + e, (z // 2) * 4 + c * 2 + z % 2))
    return lax.ppermute(jnp.concatenate([part[0], part[1]], axis=1), ("c", "u", "v"), pairs)


def slot_places(routes):
    rows = routes.shape[0]
    onehot = (routes[:, :, None] == jnp.arange(EXPERTS, dtype=jnp.int32)[None, None, :]).astype(
        jnp.int32
    )
    onehot = onehot.reshape(rows * TOP, EXPERTS)
    before = jnp.cumsum(onehot, axis=0) - onehot
    slot = jnp.sum(before * onehot, axis=1).reshape(rows, TOP)
    return routes * CAP + slot


def three_terms(values):
    high = lax.reduce_precision(values, 8, 7)
    middle = lax.reduce_precision(values - high, 8, 7)
    low = values - high - middle
    return [high, middle, low]


def neighbour(array, by):
    return lax.ppermute(array, "y", [(i, (i + by) % LANES) for i in range(LANES)])


def own_block(terms, distance):
    rows = terms.shape[0] // LANES
    place = (lax.axis_index("y") + distance) % LANES
    return lax.dynamic_slice_in_dim(terms, place * rows, rows, axis=0)


class Chain:
    def __init__(self, terms, by, length):
        self.terms, self.by, self.left = terms, by, length
        self.total = own_block(terms, by * length)

    def step(self):
        if self.left:
            self.left -= 1
            received = neighbour(self.total.astype(jnp.bfloat16), self.by).astype(jnp.float32)
            self.total = received
            if self.left:
                self.total = received + own_block(self.terms, self.by * self.left)


def slopes_kernel(e0_ref, info_ref, *refs):
    saved_refs = refs[0:4]
    slope_gate_ref, slope_up_ref = refs[4:]
    count = info_ref.shape[0]
    slots, lane = saved_refs[0].shape[0], saved_refs[0].shape[1] // 2
    facts = info_ref[...].astype(jnp.float32)
    places = [facts[:, 2:3], facts[:, 3:4]]
    gates = [
        facts[:, 4 + k : 5 + k] + facts[:, 6 + k : 7 + k] + facts[:, 8 + k : 9 + k]
        for k in range(TOP)
    ]
    source = lax.broadcasted_iota(jnp.int32, (count, 1), 0) // (count // LANES)
    start = (source * CAP + 1).astype(jnp.float32)
    spot = (lax.broadcasted_iota(jnp.int32, (1, slots), 1) + 1).astype(jnp.float32)
    for block in range(EXPERTS):
        low = ((e0_ref[0] ^ block) * CAP).astype(jnp.float32)
        weight = jnp.zeros((count, 1), jnp.float32)
        target = jnp.zeros((count, 1), jnp.float32)
        for k in range(TOP):
            named = jnp.logical_and(places[k] >= low, places[k] < low + CAP)
            weight = weight + jnp.where(named, gates[k], 0.0)
            target = target + jnp.where(named, start + places[k] - low, 0.0)
        pick = jnp.where(target == spot, 1.0, 0.0).astype(jnp.bfloat16)
        kept = jnp.dot(pick, saved_refs[block][...], preferred_element_type=jnp.float32)
        apre, bpre = kept[:, :lane], kept[:, lane:]
        sig = jax.nn.sigmoid(apre)
        columns = slice(block * lane, (block + 1) * lane)
        slope_gate_ref[:, columns] = bpre * sig * (1.0 + apre * (1.0 - sig)) * weight
        slope_up_ref[:, columns] = apre * sig * weight


def slopes(e0, gathered, width, saved):
    count = gathered.shape[0]
    half = EXPERTS * saved[0].shape[1] // 2
    info_at = 2 * width // INFO
    whole = pl.BlockSpec((count, half), lambda k: (0, 0))
    return pl.pallas_call(
        slopes_kernel,
        grid=(1,),
        in_specs=[
            pl.BlockSpec(memory_space=pltpu.SMEM),
            pl.BlockSpec((count, INFO), lambda k: (0, info_at)),
        ]
        + [pl.BlockSpec(saved[0].shape, lambda k: (0, 0))] * EXPERTS,
        out_specs=[whole, whole],
        out_shape=[jax.ShapeDtypeStruct((count, half), jnp.float32)] * 2,
        compiler_params=pltpu.CompilerParams(vmem_limit_bytes=VMEM),
        cost_estimate=pl.CostEstimate(
            flops=4 * count * half * saved[0].shape[0],
            bytes_accessed=3 << 20,
            transcendentals=count * half,
        ),
    )(e0, gathered, *saved)


def body(
    fwd_in, fwd_routes, router, bwd_in, bwd_routes, bwd_gates, w_gate, w_up, w_down, saved_pre
):
    width = fwd_in.shape[1]
    x = shift_and_swap(fwd_in, 1)
    q = shift_and_swap(bwd_in, -1)
    info = jnp.concatenate(
        [fwd_routes.astype(jnp.float32), slot_places(bwd_routes).astype(jnp.float32)]
        + three_terms(bwd_gates),
        axis=1,
    ).astype(jnp.bfloat16)
    info = swap(jnp.pad(info, ((0, 0), (0, INFO - info.shape[1]))))
    columns = swap(jnp.pad(router[0].T, ((0, 16 - EXPERTS), (0, 0))))
    after = lax.optimization_barrier
    x, q, info, columns, next_gate, next_up, next_down, kept_pre = after(
        (x, q, info, columns, w_gate[0], w_up[0], w_down[0], saved_pre[:, 0])
    )
    gathered = lax.all_gather(jnp.concatenate([x, q, info], axis=1), "y", axis=0, tiled=True)
    a0 = swap(next_gate)
    a0, next_up = after((a0, next_up))
    a1, a2, b0 = other_plane(a0), other_core(a0), swap(next_up)
    a1, b0, next_down = after((a1, b0, next_down))
    a3, b1, b2, c0 = other_core(a1), other_plane(b0), other_core(b0), swap(next_down)
    b1, c0, wg = after((b1, c0, jnp.concatenate([a0, a1, a2, a3], axis=1)))
    b3, c1, c2 = other_core(b1), other_plane(c0), other_core(c0)

    gathered = after((gathered, c0))[0]
    wu = jnp.concatenate([b0, b1, b2, b3], axis=1)
    rows = gathered[:, :width]
    grads = gathered[:, width : 2 * width]
    facts = gathered[:, 2 * width :].astype(jnp.float32)
    froutes = facts[:, 0:2].astype(jnp.int32)
    e0 = lax.axis_index("c") * 2 + lax.axis_index("v")
    lane = w_gate.shape[2]

    def per_block(routes, values):
        columns = []
        for number in range(EXPERTS):
            picked = jnp.where(routes == (e0 ^ number), values, jnp.zeros((), values.dtype))
            columns.append(jnp.sum(picked, axis=1, keepdims=True))
        return columns

    def side_by_side(columns):
        shape = (columns[0].shape[0], lane)
        return jnp.concatenate([jnp.broadcast_to(column, shape) for column in columns], axis=1)

    score = jax.nn.sigmoid(
        lax.dot_general(rows, columns, (((1,), (1,)), ((), ())), preferred_element_type=jnp.float32)
    )
    chosen = jnp.concatenate(
        [
            jnp.sum(
                jnp.where(froutes[:, k : k + 1] == jnp.arange(16)[None, :], score, 0.0),
                axis=1,
                keepdims=True,
            )
            for k in range(TOP)
        ],
        axis=1,
    )
    fgates = chosen / jnp.sum(chosen, axis=1, keepdims=True)
    fweight = side_by_side(per_block(froutes, fgates))
    gpre = jnp.dot(rows, wg, preferred_element_type=jnp.float32)
    upre = jnp.dot(rows, wu, preferred_element_type=jnp.float32)
    hidden = (jax.nn.silu(gpre) * upre * fweight).astype(jnp.bfloat16)

    c1, hidden = after((c1, hidden))
    c3 = other_core(c1)
    kept_pre = after((kept_pre, c3))[0]
    saved = [saved_of_lane(kept_pre, number) for number in range(EXPERTS)]
    wd = jnp.concatenate([c0, c1, c2, c3], axis=0)
    fpart = jnp.dot(hidden, wd, preferred_element_type=jnp.float32)
    slope_gate, slope_up = slopes(
        e0.astype(jnp.int32).reshape(1), after((gathered, hidden))[0], width, saved
    )
    dhid = lax.dot_general(
        gathered[:, width : 2 * width], wd, (((1,), (1,)), ((), ())), preferred_element_type=jnp.float32
    )
    dgate = (dhid * slope_gate).astype(jnp.bfloat16)
    dup = (dhid * slope_up).astype(jnp.bfloat16)
    ring = [Chain(fpart, 1, 4), Chain(fpart, -1, 3)]
    firsts = [chain.total.astype(jnp.bfloat16) for chain in ring]
    dgate, dup = after((dgate, dup, *firsts))[:2]
    bpart = lax.dot_general(
        dgate, wg, (((1,), (1,)), ((), ())), preferred_element_type=jnp.float32
    ) + lax.dot_general(dup, wu, (((1,), (1,)), ((), ())), preferred_element_type=jnp.float32)
    ring += [Chain(bpart, 1, 3), Chain(bpart, -1, 4)]
    for _ in range(4):
        for chain in ring:
            chain.step()
    fsum = own_block(fpart, 0) + ring[0].total + ring[1].total
    bsum = own_block(bpart, 0) + ring[2].total + ring[3].total
    fwd_out = (x.astype(jnp.float32) + fsum).astype(jnp.bfloat16)
    bwd_out = (q.astype(jnp.float32) + bsum).astype(jnp.bfloat16)
    return (swap(fwd_out), swap(bwd_out))


def solution(mesh):
    fine = Mesh(mesh.devices.reshape(SIZES), AXES)
    section = ("x", "h", "c")
    part = ("u", "v", "y")
    both = P(AXES, None)
    in_specs = (
        both,
        both,
        P(section, None, None),
        both,
        both,
        both,
        P(section, None, part),
        P(section, None, part),
        P(section, part, None),
        P(None, section, None, part),
    )
    return jax.shard_map(
        body, mesh=fine, in_specs=in_specs, out_specs=(both, both), check_vma=False
    )
```

time: 348 us -> 300 us (0.86)
  waiting for transfers between devices: 172 us -> 122 us
  starting transfers between devices: 85.6 us -> 113 us
  matrix products: 46.6 us -> 23.8 us
  local copies, waits for them, and re-layouts: 16.4 us -> 12.5 us
    reduce_scatter x2 -> x0, waiting for transfers between devices: 82.4 us -> none  [the longest x1 48.9 us: body(): fsum = lax.psum_scatter(fpart, 'y', scatter_dimension=0, tiled=True)]
    ppermute x4 -> x18, starting transfers between devices: 28.5 us -> 58.8 us  [the longest x14 46.4 us: neighbour(): lax.ppermute(array, 'y', [(i, (i + by) % LANES) for i in range(LANES)])]
    ppermute x4 -> x18, waiting for transfers between devices: 6.47 us -> 29.1 us  [the longest x14 29.1 us: neighbour(): lax.ppermute(array, 'y', [(i, (i + by) % LANES) for i in range(LANES)])]
    dot_general x18 -> x6, matrix products: 43.5 us -> 22.7 us  [the longest x1 6.43 us: body(): gpre = jnp.dot(rows, wg, preferred_element_type=jnp.float32)]
    ppermute x6 -> x7, waiting for transfers between devices: 35.2 us -> 49 us  [swap(): return lax.ppermute(array, ('c', 'u'), [(0, 0), (1, 2), (2, 1), (3, 3)])]
    all_gather x2 -> x1, waiting for transfers between devices: 9.52 us -> 0.01 us  [body(): lax.all_gather(jnp.concatenate([x, q, info], axis=1), 'y', axis=0, tiled=...]
    gather x3 -> x0, local copies, waits for them, and re-layouts: 9.43 us -> none  [body(): chosen = jnp.take_along_axis(score, froutes, axis=1)]
    ppermute x2, starting transfers between devices: 22.7 us -> 13.9 us  [shift_and_swap(): return lax.ppermute(array, ('x', 'h', 'c', 'u'), pairs)]
  transfers between devices with their start and end apart: 22 -> 37, of which waited for: 11 -> 19; matrix products, arithmetic and copies ran while one was open for 18% -> 15% of each run, Pallas kernels for 0% -> 1%
where the time goes in v2:
time: 300 us; the launch traced here: 297 us
  waiting for transfers between devices  122 us (41%)
  starting transfers between devices  113 us (38%)
  matrix products  23.8 us (8%)
  between operations  14.9 us (5%)
  local copies, waits for them, and re-layouts  12.5 us (4%)
  other arithmetic  10 us (3%)
    ppermute x7, waiting for transfers between devices, swap(): return lax.ppermute(array, ('c', 'u'), [(0, 0), (1, 2), (2, 1), (3, 3)])  49 us
    ppermute x14, starting transfers between devices, neighbour(): lax.ppermute(array, 'y', [(i, (i + by) % LANES) for i in range(LANES)])  46.4 us
    ppermute x3, waiting for transfers between devices, other_plane(): return lax.ppermute(array, 'v', [(0, 1), (1, 0)])  35.3 us
    ppermute x14, waiting for transfers between devices, neighbour(): lax.ppermute(array, 'y', [(i, (i + by) % LANES) for i in range(LANES)])  29.1 us
    ppermute x7, starting transfers between devices, swap(): return lax.ppermute(array, ('c', 'u'), [(0, 0), (1, 2), (2, 1), (3, 3)])  20.1 us
    ppermute x2, starting transfers between devices, shift_and_swap(): return lax.ppermute(array, ('x', 'h', 'c', 'u'), pairs)  13.9 us
    ppermute x6, starting transfers between devices, other_core(): return lax.ppermute(array, 'c', [(0, 1), (1, 0)])  13.4 us
    ppermute x4, starting transfers between devices, saved_of_lane(): lax.ppermute(jnp.concatenate([part[0], part[1]], axis=1), ('c', 'u', 'v')...  12.4 us
  transfers between devices with their start and end apart: 37, of which 19 were waited for; matrix products, arithmetic and copies ran while one was open for 15% of the time, Pallas kernels for 1%

profile of v2, /device:TPU:1, one launch (start us, length us, event | category | flops | bytes accessed | tf_op | source)
XLA Modules:
  0.0 297.5 jit_solution(18098428442992875506)
XLA Ops:
  7.2 12.0 %collective-permute-start = (bf16[64,3584]{1,0:T(8,128)(2,1)}, bf16[64,3584]{1,0:T(8,128)(2,1)S(1)}, u32[]{:S(2)}, u32[]{:S(2)}) collective-permute-start(bf16[64,3584]{1,0:T(8,128)(2,1)} %param.10), channel_id=1, source_target_pairs={{0,16},{16,48},{32,64},{48,96},{64,80},{80,112},{96,128},{112,160}... | collective-permute-start | bytes 1376264 | tf_op jit(solution)/shard_map/ppermute | solution.py:31
  21.9 5.9 %collective-permute-start.3 = (bf16[16,3584]{1,0:T(8,128)(2,1)S(1)}, bf16[16,3584]{1,0:T(8,128)(2,1)S(1)}, u32[]{:S(2)}, u32[]{:S(2)}) collective-permute-start(bf16[16,3584]{1,0:T(8,128)(2,1)S(1)} %pad.9), channel_id=1, source_target_pairs={{0,0},{16,32},{32,16},{48,48},{1,1},{17,33},{33,17},{49,49},{2,2},... | collective-permute-start | bytes 344072 | tf_op jit(solution)/shard_map/ppermute | solution.py:20
  32.9 4.4 %collective-permute-done.2 = bf16[64,128]{1,0:T(8,128)(2,1)S(1)} collective-permute-done((bf16[64,128]{1,0:T(8,128)(2,1)S(1)}, bf16[64,128]{1,0:T(8,128)(2,1)S(1)}, u32[]{:S(2)}, u32[]{:S(2)}) %collective-permute-start.2) | collective-permute-done | bytes 16416 | tf_op jit(solution)/shard_map/ppermute | solution.py:20
  37.3 6.6 %collective-permute-done.1 = bf16[64,3584]{1,0:T(8,128)(2,1)S(1)} collective-permute-done((bf16[64,3584]{1,0:T(8,128)(2,1)}, bf16[64,3584]{1,0:T(8,128)(2,1)S(1)}, u32[]{:S(2)}, u32[]{:S(2)}) %collective-permute-start.1) | collective-permute-done | bytes 458784 | tf_op jit(solution)/shard_map/ppermute | solution.py:31
  45.0 1.9 collective-permute-start.4
  46.9 23.3 %collective-permute-done.4 = bf16[3584,128]{1,0:T(8,128)(2,1)S(1)} collective-permute-done((bf16[3584,128]{1,0:T(8,128)(2,1)}, bf16[3584,128]{1,0:T(8,128)(2,1)S(1)}, u32[]{:S(2)}, u32[]{:S(2)}) %collective-permute-start.4) | collective-permute-done | bytes 917536 | tf_op jit(solution)/shard_map/ppermute | solution.py:20
  72.1 1.9 collective-permute-start.6
  74.0 1.9 collective-permute-start.9
  76.0 14.9 %collective-permute-done.5 = bf16[3584,128]{1,0:T(8,128)(2,1)S(1)} collective-permute-done((bf16[3584,128]{1,0:T(8,128)(2,1)S(1)}, bf16[3584,128]{1,0:T(8,128)(2,1)S(1)}, u32[]{:S(2)}, u32[]{:S(2)}) %collective-permute-start.5) | collective-permute-done | bytes 917536 | tf_op jit(solution)/shard_map/ppermute | solution.py:35
  90.8 7.4 %collective-permute-done.6 = bf16[3584,128]{1,0:T(8,128)(2,1)} collective-permute-done((bf16[3584,128]{1,0:T(8,128)(2,1)}, bf16[3584,128]{1,0:T(8,128)(2,1)}, u32[]{:S(2)}, u32[]{:S(2)}) %collective-permute-start.6) | collective-permute-done | bytes 917536 | tf_op jit(solution)/shard_map/ppermute | solution.py:20
  102.2 2.4 collective-permute-start.12
  104.7 3.1 %collective-permute-start.8 = (bf16[128,3584]{1,0:T(8,128)(2,1)}, bf16[128,3584]{1,0:T(8,128)(2,1)}, u32[]{:S(2)}, u32[]{:S(2)}) collective-permute-start(bf16[128,3584]{1,0:T(8,128)(2,1)} %bitcast.46), channel_id=1, source_target_pairs={{0,0},{16,32},{32,16},{48,48},{1,1},{17,33},{33,17},{49,49},{2,2},... | collective-permute-start | bytes 2752520 | tf_op jit(solution)/shard_map/ppermute | solution.py:20
  107.7 2.2 constant_dynamic-update-slice_fusion.3
  109.9 3.3 %pad_maximum_fusion = bf16[3584,512]{1,0:T(8,128)(2,1)} fusion(bf16[3584,128]{1,0:T(8,128)(2,1)} %collective-permute-done.10, bf16[3584,128]{1,0:T(8,128)(2,1)} %collective-permute-done.9, bf16[3584,128]{1,0:T(8,128)(2,1)S(1)} %collective-permute-done.5, bf16[3584,128]{1,0:T(8,128)(2,1)S(1)} %collective-permute-done.4), kind=kLoop, calls=%fused_computation.1 | loop fusion | flops 14680064 | bytes 7340032 | tf_op jit(solution)/shard_map/concatenate | solution.py:174
  113.2 20.5 %collective-permute-done.7 = bf16[3584,128]{1,0:T(8,128)(2,1)S(1)} collective-permute-done((bf16[3584,128]{1,0:T(8,128)(2,1)}, bf16[3584,128]{1,0:T(8,128)(2,1)S(1)}, u32[]{:S(2)}, u32[]{:S(2)}) %collective-permute-start.7) | collective-permute-done | bytes 917536 | tf_op jit(solution)/shard_map/ppermute | solution.py:35
  133.7 2.5 collective-permute-start.11
  136.1 2.7 collective-permute-start.14
  138.8 1.9 collective-permute-start.13
  140.8 2.2 constant_dynamic-update-slice_fusion.7
  147.2 6.4 %fusion.6 = f32[512,512]{1,0:T(8,128)} fusion(bf16[3584,512]{1,0:T(8,128)(2,1)} %pad_maximum_fusion, bf16[512,7296]{1,0:T(8,128)(2,1)} %all-gather.2.cloned.1.call-done.info_ref), kind=kOutput, calls=%fused_computation.8 | convolution fusion | flops 1879048192 | bytes 8388608 | tf_op jit(solution)/shard_map/dot_general | solution.py:213
  157.1 5.7 %fusion.20 = bf16[512,512]{1,0:T(8,128)(2,1)S(1)} fusion(f32[512,128]{1,0:T(8,128)S(1)} %broadcast_in_dim.54, f32[512,128]{1,0:T(8,128)S(1)} %broadcast_in_dim.53, f32[512,128]{1,0:T(8,128)S(1)} %broadcast_in_dim.52, f32[512,128]{1,0:T(8,128)S(1)} %broadcast_in_dim.51, f32[512,512]{1,0:T(8,128)} %fusion.6, ...), kind=kOutput, calls=%fused_computation.15 | convolution fusion | flops 1881669632 | bytes 9961472 | tf_op jit(solution)/shard_map/dot_general | solution.py:214
  162.9 2.5 collective-permute-start.15
  167.6 4.4 %collective-permute-start.27 = (bf16[272,256]{1,0:T(8,128)(2,1)S(1)}, bf16[272,256]{1,0:T(8,128)(2,1)S(1)}, u32[]{:S(2)}, u32[]{:S(2)}) collective-permute-start(bf16[272,256]{1,0:T(8,128)(2,1)S(1)} %pad_maximum_fusion.5), channel_id=1, source_target_pairs={{0,40},{8,32},{16,8},{24,0},{32,56},{40,48},{48,24},{56,16},{1,41}... | collective-permute-start | bytes 417800 | tf_op jit(solution)/shard_map/ppermute | solution.py:51
  172.0 2.5 collective-permute-start.26
  174.5 3.3 %collective-permute-start.25 = (bf16[272,256]{1,0:T(8,128)(2,1)S(1)}, bf16[272,256]{1,0:T(8,128)(2,1)S(1)}, u32[]{:S(2)}, u32[]{:S(2)}) collective-permute-start(bf16[272,256]{1,0:T(8,128)(2,1)S(1)} %pad_maximum_fusion.3), channel_id=1, source_target_pairs={{0,8},{8,0},{16,40},{24,32},{32,24},{40,16},{48,56},{56,48},{1,9},... | collective-permute-start | bytes 417800 | tf_op jit(solution)/shard_map/ppermute | solution.py:51
  177.8 2.3 collective-permute-start.24
  180.1 2.1 fusion.27
  182.3 3.0 %collective-permute-start.16 = (bf16[64,3584]{1,0:T(8,128)(2,1)S(1)}, bf16[64,3584]{1,0:T(8,128)(2,1)S(1)}, u32[]{:S(2)}, u32[]{:S(2)}) collective-permute-start(bf16[64,3584]{1,0:T(8,128)(2,1)S(1)} %get-tuple-element.70), channel_id=1, source_target_pairs={{0,1},{1,2},{2,3},{3,4},{4,5},{5,6},{6,7},{7,0},{8,9},{9,10},{10,1... | collective-permute-start | bytes 1376264 | tf_op jit(solution)/shard_map/ppermute | solution.py:73
  185.3 4.2 %collective-permute-start.20 = (bf16[64,3584]{1,0:T(8,128)(2,1)S(1)}, bf16[64,3584]{1,0:T(8,128)(2,1)S(1)}, u32[]{:S(2)}, u32[]{:S(2)}) collective-permute-start(bf16[64,3584]{1,0:T(8,128)(2,1)S(1)} %get-tuple-element.71), channel_id=1, source_target_pairs={{0,7},{1,0},{2,1},{3,2},{4,3},{5,4},{6,5},{7,6},{8,15},{9,8},{10,9... | collective-permute-start | bytes 1376264 | tf_op jit(solution)/shard_map/ppermute | solution.py:73
  191.3 2.1 multiply_convert_fusion
  193.4 4.3 %fusion.28 = f32[512,3584]{1,0:T(8,128)S(1)} fusion(bf16[512,512]{1,0:T(8,128)(2,1)S(1)} %get-tuple-element.51, bf16[3584,512]{1,0:T(8,128)(2,1)} %constant_dynamic-update-slice_fusion), kind=kOutput, calls=%fused_computation.83 | convolution fusion | flops 1879048192 | bytes 11534336 | tf_op jit(solution)/shard_map/dot_general | solution.py:236
  197.7 2.1 convolution_add_fusion
  199.9 3.4 %collective-permute-start.31 = (bf16[64,3584]{1,0:T(8,128)(2,1)S(1)}, bf16[64,3584]{1,0:T(8,128)(2,1)S(1)}, u32[]{:S(2)}, u32[]{:S(2)}) collective-permute-start(bf16[64,3584]{1,0:T(8,128)(2,1)S(1)} %get-tuple-element.65), channel_id=1, source_target_pairs={{0,7},{1,0},{2,1},{3,2},{4,3},{5,4},{6,5},{7,6},{8,15},{9,8},{10,9... | collective-permute-start | bytes 1376264 | tf_op jit(solution)/shard_map/ppermute | solution.py:73
  203.3 1.9 collective-permute-start.28
  207.2 4.9 %collective-permute-done.31 = bf16[64,3584]{1,0:T(8,128)(2,1)S(1)} collective-permute-done((bf16[64,3584]{1,0:T(8,128)(2,1)S(1)}, bf16[64,3584]{1,0:T(8,128)(2,1)S(1)}, u32[]{:S(2)}, u32[]{:S(2)}) %collective-permute-start.31) | collective-permute-done | bytes 458784 | tf_op jit(solution)/shard_map/ppermute | solution.py:73
  212.2 4.6 %collective-permute-start.32 = (bf16[64,3584]{1,0:T(8,128)(2,1)S(1)}, bf16[64,3584]{1,0:T(8,128)(2,1)S(1)}, u32[]{:S(2)}, u32[]{:S(2)}) collective-permute-start(bf16[64,3584]{1,0:T(8,128)(2,1)S(1)} %add_convert_fusion.3), channel_id=1, source_target_pairs={{0,7},{1,0},{2,1},{3,2},{4,3},{5,4},{6,5},{7,6},{8,15},{9,8},{10,9... | collective-permute-start | bytes 1376264 | tf_op jit(solution)/shard_map/ppermute | solution.py:73
  216.8 10.0 %collective-permute-done.17 = bf16[64,3584]{1,0:T(8,128)(2,1)S(1)} collective-permute-done((bf16[64,3584]{1,0:T(8,128)(2,1)S(1)}, bf16[64,3584]{1,0:T(8,128)(2,1)S(1)}, u32[]{:S(2)}, u32[]{:S(2)}) %collective-permute-start.17) | collective-permute-done | bytes 458784 | tf_op jit(solution)/shard_map/ppermute | solution.py:73
  228.9 4.6 %collective-permute-start.21 = (bf16[64,3584]{1,0:T(8,128)(2,1)S(1)}, bf16[64,3584]{1,0:T(8,128)(2,1)S(1)}, u32[]{:S(2)}, u32[]{:S(2)}) collective-permute-start(bf16[64,3584]{1,0:T(8,128)(2,1)S(1)} %get-tuple-element.69), channel_id=1, source_target_pairs={{0,7},{1,0},{2,1},{3,2},{4,3},{5,4},{6,5},{7,6},{8,15},{9,8},{10,9... | collective-permute-start | bytes 1376264 | tf_op jit(solution)/shard_map/ppermute | solution.py:73
  235.6 4.6 %collective-permute-start.33 = (bf16[64,3584]{1,0:T(8,128)(2,1)S(1)}, bf16[64,3584]{1,0:T(8,128)(2,1)S(1)}, u32[]{:S(2)}, u32[]{:S(2)}) collective-permute-start(bf16[64,3584]{1,0:T(8,128)(2,1)S(1)} %get-tuple-element.63), channel_id=1, source_target_pairs={{0,7},{1,0},{2,1},{3,2},{4,3},{5,4},{6,5},{7,6},{8,15},{9,8},{10,9... | collective-permute-start | bytes 1376264 | tf_op jit(solution)/shard_map/ppermute | solution.py:73
  240.2 2.3 collective-permute-done.18
  244.0 1.9 collective-permute-start.19
  245.9 5.3 %collective-permute-start.22 = (bf16[64,3584]{1,0:T(8,128)(2,1)S(1)}, bf16[64,3584]{1,0:T(8,128)(2,1)S(1)}, u32[]{:S(2)}, u32[]{:S(2)}) collective-permute-start(bf16[64,3584]{1,0:T(8,128)(2,1)S(1)} %get-tuple-element.67), channel_id=1, source_target_pairs={{0,7},{1,0},{2,1},{3,2},{4,3},{5,4},{6,5},{7,6},{8,15},{9,8},{10,9... | collective-permute-start | bytes 1376264 | tf_op jit(solution)/shard_map/ppermute | solution.py:73
  255.7 5.3 %collective-permute-start.34 = (bf16[64,3584]{1,0:T(8,128)(2,1)S(1)}, bf16[64,3584]{1,0:T(8,128)(2,1)S(1)}, u32[]{:S(2)}, u32[]{:S(2)}) collective-permute-start(bf16[64,3584]{1,0:T(8,128)(2,1)S(1)} %get-tuple-element.61), channel_id=1, source_target_pairs={{0,7},{1,0},{2,1},{3,2},{4,3},{5,4},{6,5},{7,6},{8,15},{9,8},{10,9... | collective-permute-start | bytes 1376264 | tf_op jit(solution)/shard_map/ppermute | solution.py:73
  263.7 3.5 %collective-permute-start.23 = (bf16[64,3584]{1,0:T(8,128)(2,1)S(1)}, bf16[64,3584]{1,0:T(8,128)(2,1)S(1)}, u32[]{:S(2)}, u32[]{:S(2)}) collective-permute-start(bf16[64,3584]{1,0:T(8,128)(2,1)S(1)} %add_convert_fusion.6), channel_id=1, source_target_pairs={{0,0},{16,32},{32,16},{48,48},{1,1},{17,33},{33,17},{49,49},{2,2},... | collective-permute-start | bytes 1376264 | tf_op jit(solution)/shard_map/ppermute | solution.py:20
  267.1 4.1 %collective-permute-done.30 = bf16[64,3584]{1,0:T(8,128)(2,1)S(1)} collective-permute-done((bf16[64,3584]{1,0:T(8,128)(2,1)S(1)}, bf16[64,3584]{1,0:T(8,128)(2,1)S(1)}, u32[]{:S(2)}, u32[]{:S(2)}) %collective-permute-start.30) | collective-permute-done | bytes 458784 | tf_op jit(solution)/shard_map/ppermute | solution.py:73
  273.2 1.9 collective-permute-start.35
  275.1 4.2 %collective-permute-done.23 = bf16[64,3584]{1,0:T(8,128)(2,1)S(1)} collective-permute-done((bf16[64,3584]{1,0:T(8,128)(2,1)S(1)}, bf16[64,3584]{1,0:T(8,128)(2,1)S(1)}, u32[]{:S(2)}, u32[]{:S(2)}) %collective-permute-start.23) | collective-permute-done | bytes 458784 | tf_op jit(solution)/shard_map/ppermute | solution.py:20
  279.3 9.8 %collective-permute-done.35 = bf16[64,3584]{1,0:T(8,128)(2,1)S(1)} collective-permute-done((bf16[64,3584]{1,0:T(8,128)(2,1)S(1)}, bf16[64,3584]{1,0:T(8,128)(2,1)S(1)}, u32[]{:S(2)}, u32[]{:S(2)}) %collective-permute-start.35) | collective-permute-done | bytes 458784 | tf_op jit(solution)/shard_map/ppermute | solution.py:20
  (101 shorter events, 44.7 us)
Async XLA Ops:
  7.2 138.9 %all-gather.2.cloned.1.call-start = ((), (), s32[]{:S(2)}) async-start(), calls=%async_computation | async-start | bytes 8404992 | tf_op jit(solution)/shard_map/all_gather | solution.py:168
  7.2 30.1 %collective-permute-start = (bf16[64,3584]{1,0:T(8,128)(2,1)}, bf16[64,3584]{1,0:T(8,128)(2,1)S(1)}, u32[]{:S(2)}, u32[]{:S(2)}) collective-permute-start(bf16[64,3584]{1,0:T(8,128)(2,1)} %param.10), channel_id=1, source_target_pairs={{0,16},{16,48},{32,64},{48,96},{64,80},{80,112},{96,128},{112,160}... | collective-permute-start | bytes 1376264 | tf_op jit(solution)/shard_map/ppermute | solution.py:31
  19.2 24.7 %collective-permute-start.1 = (bf16[64,3584]{1,0:T(8,128)(2,1)}, bf16[64,3584]{1,0:T(8,128)(2,1)S(1)}, u32[]{:S(2)}, u32[]{:S(2)}) collective-permute-start(bf16[64,3584]{1,0:T(8,128)(2,1)} %param.13), channel_id=1, source_target_pairs={{0,464},{16,496},{32,0},{48,32},{64,16},{80,48},{96,64},{112,96},{... | collective-permute-start | bytes 1376264 | tf_op jit(solution)/shard_map/ppermute | solution.py:31
  21.9 15.4 %collective-permute-start.3 = (bf16[16,3584]{1,0:T(8,128)(2,1)S(1)}, bf16[16,3584]{1,0:T(8,128)(2,1)S(1)}, u32[]{:S(2)}, u32[]{:S(2)}) collective-permute-start(bf16[16,3584]{1,0:T(8,128)(2,1)S(1)} %pad.9), channel_id=1, source_target_pairs={{0,0},{16,32},{32,16},{48,48},{1,1},{17,33},{33,17},{49,49},{2,2},... | collective-permute-start | bytes 344072 | tf_op jit(solution)/shard_map/ppermute | solution.py:20
  31.0 6.3 %collective-permute-start.2 = (bf16[64,128]{1,0:T(8,128)(2,1)S(1)}, bf16[64,128]{1,0:T(8,128)(2,1)S(1)}, u32[]{:S(2)}, u32[]{:S(2)}) collective-permute-start(bf16[64,128]{1,0:T(8,128)(2,1)S(1)} %pad.8), channel_id=1, source_target_pairs={{0,0},{16,32},{32,16},{48,48},{1,1},{17,33},{33,17},{49,49},{2,2},... | collective-permute-start | bytes 49160 | tf_op jit(solution)/shard_map/ppermute | solution.py:20
  45.0 25.2 %collective-permute-start.4 = (bf16[3584,128]{1,0:T(8,128)(2,1)}, bf16[3584,128]{1,0:T(8,128)(2,1)S(1)}, u32[]{:S(2)}, u32[]{:S(2)}) collective-permute-start(bf16[3584,128]{1,0:T(8,128)(2,1)} %bitcast.44), channel_id=1, source_target_pairs={{0,0},{16,32},{32,16},{48,48},{1,1},{17,33},{33,17},{49,49},{2,2},... | collective-permute-start | bytes 2752520 | tf_op jit(solution)/shard_map/ppermute | solution.py:20
  70.2 20.6 %collective-permute-start.5 = (bf16[3584,128]{1,0:T(8,128)(2,1)S(1)}, bf16[3584,128]{1,0:T(8,128)(2,1)S(1)}, u32[]{:S(2)}, u32[]{:S(2)}) collective-permute-start(bf16[3584,128]{1,0:T(8,128)(2,1)S(1)} %collective-permute-done.4), channel_id=1, source_target_pairs={{0,8},{8,0},{1,9},{9,1},{2,10},{10,2},{3,11},{11,3},{4,12},{12,4},... | collective-permute-start | bytes 2752520 | tf_op jit(solution)/shard_map/ppermute | solution.py:35
  72.1 26.1 %collective-permute-start.6 = (bf16[3584,128]{1,0:T(8,128)(2,1)}, bf16[3584,128]{1,0:T(8,128)(2,1)}, u32[]{:S(2)}, u32[]{:S(2)}) collective-permute-start(bf16[3584,128]{1,0:T(8,128)(2,1)} %bitcast.45), channel_id=1, source_target_pairs={{0,0},{16,32},{32,16},{48,48},{1,1},{17,33},{33,17},{49,49},{2,2},... | collective-permute-start | bytes 2752520 | tf_op jit(solution)/shard_map/ppermute | solution.py:20
  74.0 35.9 %collective-permute-start.9 = (bf16[3584,128]{1,0:T(8,128)(2,1)S(1)}, bf16[3584,128]{1,0:T(8,128)(2,1)}, u32[]{:S(2)}, u32[]{:S(2)}) collective-permute-start(bf16[3584,128]{1,0:T(8,128)(2,1)S(1)} %collective-permute-done.4), channel_id=1, source_target_pairs={{0,32},{32,0},{1,33},{33,1},{2,34},{34,2},{3,35},{35,3},{4,36},{36... | collective-permute-start | bytes 2752520 | tf_op jit(solution)/shard_map/ppermute | solution.py:39
  98.2 11.7 %collective-permute-start.10 = (bf16[3584,128]{1,0:T(8,128)(2,1)S(1)}, bf16[3584,128]{1,0:T(8,128)(2,1)}, u32[]{:S(2)}, u32[]{:S(2)}) collective-permute-start(bf16[3584,128]{1,0:T(8,128)(2,1)S(1)} %collective-permute-done.5), channel_id=1, source_target_pairs={{0,32},{32,0},{1,33},{33,1},{2,34},{34,2},{3,35},{35,3},{4,36},{36... | collective-permute-start | bytes 2752520 | tf_op jit(solution)/shard_map/ppermute | solution.py:39
  100.3 33.4 %collective-permute-start.7 = (bf16[3584,128]{1,0:T(8,128)(2,1)}, bf16[3584,128]{1,0:T(8,128)(2,1)S(1)}, u32[]{:S(2)}, u32[]{:S(2)}) collective-permute-start(bf16[3584,128]{1,0:T(8,128)(2,1)} %collective-permute-done.6), channel_id=1, source_target_pairs={{0,8},{8,0},{1,9},{9,1},{2,10},{10,2},{3,11},{11,3},{4,12},{12,4},... | collective-permute-start | bytes 2752520 | tf_op jit(solution)/shard_map/ppermute | solution.py:35
  102.2 41.8 %collective-permute-start.12 = (bf16[3584,128]{1,0:T(8,128)(2,1)}, bf16[3584,128]{1,0:T(8,128)(2,1)S(1)}, u32[]{:S(2)}, u32[]{:S(2)}) collective-permute-start(bf16[3584,128]{1,0:T(8,128)(2,1)} %collective-permute-done.6), channel_id=1, source_target_pairs={{0,32},{32,0},{1,33},{33,1},{2,34},{34,2},{3,35},{35,3},{4,36},{36... | collective-permute-start | bytes 2752520 | tf_op jit(solution)/shard_map/ppermute | solution.py:39
  104.7 29.0 %collective-permute-start.8 = (bf16[128,3584]{1,0:T(8,128)(2,1)}, bf16[128,3584]{1,0:T(8,128)(2,1)}, u32[]{:S(2)}, u32[]{:S(2)}) collective-permute-start(bf16[128,3584]{1,0:T(8,128)(2,1)} %bitcast.46), channel_id=1, source_target_pairs={{0,0},{16,32},{32,16},{48,48},{1,1},{17,33},{33,17},{49,49},{2,2},... | collective-permute-start | bytes 2752520 | tf_op jit(solution)/shard_map/ppermute | solution.py:20
  133.7 29.2 %collective-permute-start.11 = (bf16[128,3584]{1,0:T(8,128)(2,1)}, bf16[128,3584]{1,0:T(8,128)(2,1)S(1)}, u32[]{:S(2)}, u32[]{:S(2)}) collective-permute-start(bf16[128,3584]{1,0:T(8,128)(2,1)} %collective-permute-done.8), channel_id=1, source_target_pairs={{0,8},{8,0},{1,9},{9,1},{2,10},{10,2},{3,11},{11,3},{4,12},{12,4},... | collective-permute-start | bytes 2752520 | tf_op jit(solution)/shard_map/ppermute | solution.py:35
  136.1 29.3 %collective-permute-start.14 = (bf16[128,3584]{1,0:T(8,128)(2,1)}, bf16[128,3584]{1,0:T(8,128)(2,1)S(1)}, u32[]{:S(2)}, u32[]{:S(2)}) collective-permute-start(bf16[128,3584]{1,0:T(8,128)(2,1)} %collective-permute-done.8), channel_id=1, source_target_pairs={{0,32},{32,0},{1,33},{33,1},{2,34},{34,2},{3,35},{35,3},{4,36},{36... | collective-permute-start | bytes 2752520 | tf_op jit(solution)/shard_map/ppermute | solution.py:39
  138.8 6.2 %collective-permute-start.13 = (bf16[3584,128]{1,0:T(8,128)(2,1)S(1)}, bf16[3584,128]{1,0:T(8,128)(2,1)S(1)}, u32[]{:S(2)}, u32[]{:S(2)}) collective-permute-start(bf16[3584,128]{1,0:T(8,128)(2,1)S(1)} %collective-permute-done.7), channel_id=1, source_target_pairs={{0,32},{32,0},{1,33},{33,1},{2,34},{34,2},{3,35},{35,3},{4,36},{36... | collective-permute-start | bytes 2752520 | tf_op jit(solution)/shard_map/ppermute | solution.py:39
  146.1 7.8 %slice-start = ((s8[7471104]{0:T(1024)(128)(4,1)}), s8[4194304]{0:T(1024)(128)(4,1)S(1)}, s32[]{:S(2)}) async-start(s8[7471104]{0:T(1024)(128)(4,1)} %bitcast.36), calls=%async_computation.1 | async-start | bytes 8388608
  147.2 6.8 %slice-start.1 = ((s8[7471104]{0:T(1024)(128)(4,1)}), s8[3276800]{0:T(1024)(128)(4,1)S(1)}, s32[]{:S(2)}) async-start(s8[7471104]{0:T(1024)(128)(4,1)} %bitcast.36), calls=%async_computation.2 | async-start | bytes 6553600
  157.1 8.3 %copy-start.1 = (bf16[512,3584]{1,0:T(8,128)(2,1)S(1)}, bf16[512,3584]{1,0:T(8,128)(2,1)}, u32[]{:S(2)}) copy-start(bf16[512,3584]{1,0:T(8,128)(2,1)} %constant_dynamic-update-slice_fusion.7) | copy-start | bytes 11010052
  162.8 4.6 %copy-start.2 = (bf16[2,1,1088,128]{3,2,1,0:T(8,128)(2,1)S(1)}, bf16[2,1,1088,128]{3,2,1,0:T(8,128)(2,1)}, u32[]{:S(2)}) copy-start(bf16[2,1,1088,128]{3,2,1,0:T(8,128)(2,1)} %param.19) | copy-start | bytes 1671172
  162.9 4.6 %collective-permute-start.15 = (bf16[128,3584]{1,0:T(8,128)(2,1)S(1)}, bf16[128,3584]{1,0:T(8,128)(2,1)S(1)}, u32[]{:S(2)}, u32[]{:S(2)}) collective-permute-start(bf16[128,3584]{1,0:T(8,128)(2,1)S(1)} %collective-permute-done.11), channel_id=1, source_target_pairs={{0,32},{32,0},{1,33},{33,1},{2,34},{34,2},{3,35},{35,3},{4,36},{36... | collective-permute-start | bytes 2752520 | tf_op jit(solution)/shard_map/ppermute | solution.py:39
  167.6 17.8 %collective-permute-start.27 = (bf16[272,256]{1,0:T(8,128)(2,1)S(1)}, bf16[272,256]{1,0:T(8,128)(2,1)S(1)}, u32[]{:S(2)}, u32[]{:S(2)}) collective-permute-start(bf16[272,256]{1,0:T(8,128)(2,1)S(1)} %pad_maximum_fusion.5), channel_id=1, source_target_pairs={{0,40},{8,32},{16,8},{24,0},{32,56},{40,48},{48,24},{56,16},{1,41}... | collective-permute-start | bytes 417800 | tf_op jit(solution)/shard_map/ppermute | solution.py:51
  172.0 17.6 %collective-permute-start.26 = (bf16[272,256]{1,0:T(8,128)(2,1)S(1)}, bf16[272,256]{1,0:T(8,128)(2,1)S(1)}, u32[]{:S(2)}, u32[]{:S(2)}) collective-permute-start(bf16[272,256]{1,0:T(8,128)(2,1)S(1)} %pad_maximum_fusion.4), channel_id=1, source_target_pairs={{0,32},{8,40},{16,0},{24,8},{32,48},{40,56},{48,16},{56,24},{1,33}... | collective-permute-start | bytes 417800 | tf_op jit(solution)/shard_map/ppermute | solution.py:51
  174.5 15.1 %collective-permute-start.25 = (bf16[272,256]{1,0:T(8,128)(2,1)S(1)}, bf16[272,256]{1,0:T(8,128)(2,1)S(1)}, u32[]{:S(2)}, u32[]{:S(2)}) collective-permute-start(bf16[272,256]{1,0:T(8,128)(2,1)S(1)} %pad_maximum_fusion.3), channel_id=1, source_target_pairs={{0,8},{8,0},{16,40},{24,32},{32,24},{40,16},{48,56},{56,48},{1,9},... | collective-permute-start | bytes 417800 | tf_op jit(solution)/shard_map/ppermute | solution.py:51
  177.8 11.8 %collective-permute-start.24 = (bf16[272,256]{1,0:T(8,128)(2,1)S(1)}, bf16[272,256]{1,0:T(8,128)(2,1)S(1)}, u32[]{:S(2)}, u32[]{:S(2)}) collective-permute-start(bf16[272,256]{1,0:T(8,128)(2,1)S(1)} %pad_maximum_fusion.2), channel_id=1, source_target_pairs={{0,0},{8,8},{16,32},{24,40},{32,16},{40,24},{48,48},{56,56},{1,1},... | collective-permute-start | bytes 417800 | tf_op jit(solution)/shard_map/ppermute | solution.py:51
  180.0 9.5 %slice-start.2 = ((s8[7471104]{0:T(1024)(128)(4,1)}), s8[4194304]{0:T(1024)(128)(4,1)S(1)}, s32[]{:S(2)}) async-start(s8[7471104]{0:T(1024)(128)(4,1)} %bitcast.38), calls=%async_computation.3 | async-start | bytes 8388608
  180.1 9.5 %slice-start.3 = ((s8[7471104]{0:T(1024)(128)(4,1)}), s8[3276800]{0:T(1024)(128)(4,1)S(1)}, s32[]{:S(2)}) async-start(s8[7471104]{0:T(1024)(128)(4,1)} %bitcast.38), calls=%async_computation.4 | async-start | bytes 6553600
  182.3 22.9 %collective-permute-start.16 = (bf16[64,3584]{1,0:T(8,128)(2,1)S(1)}, bf16[64,3584]{1,0:T(8,128)(2,1)S(1)}, u32[]{:S(2)}, u32[]{:S(2)}) collective-permute-start(bf16[64,3584]{1,0:T(8,128)(2,1)S(1)} %get-tuple-element.70), channel_id=1, source_target_pairs={{0,1},{1,2},{2,3},{3,4},{4,5},{5,6},{6,7},{7,0},{8,9},{9,10},{10,1... | collective-permute-start | bytes 1376264 | tf_op jit(solution)/shard_map/ppermute | solution.py:73
  185.3 31.4 %collective-permute-start.20 = (bf16[64,3584]{1,0:T(8,128)(2,1)S(1)}, bf16[64,3584]{1,0:T(8,128)(2,1)S(1)}, u32[]{:S(2)}, u32[]{:S(2)}) collective-permute-start(bf16[64,3584]{1,0:T(8,128)(2,1)S(1)} %get-tuple-element.71), channel_id=1, source_target_pairs={{0,7},{1,0},{2,1},{3,2},{4,3},{5,4},{6,5},{7,6},{8,15},{9,8},{10,9... | collective-permute-start | bytes 1376264 | tf_op jit(solution)/shard_map/ppermute | solution.py:73
  193.4 4.3 %copy-start = (bf16[3584,512]{1,0:T(8,128)(2,1)S(1)}, bf16[3584,512]{1,0:T(8,128)(2,1)}, u32[]{:S(2)}) copy-start(bf16[3584,512]{1,0:T(8,128)(2,1)} %pad_maximum_fusion) | copy-start | bytes 11010052
  199.9 12.2 %collective-permute-start.31 = (bf16[64,3584]{1,0:T(8,128)(2,1)S(1)}, bf16[64,3584]{1,0:T(8,128)(2,1)S(1)}, u32[]{:S(2)}, u32[]{:S(2)}) collective-permute-start(bf16[64,3584]{1,0:T(8,128)(2,1)S(1)} %get-tuple-element.65), channel_id=1, source_target_pairs={{0,7},{1,0},{2,1},{3,2},{4,3},{5,4},{6,5},{7,6},{8,15},{9,8},{10,9... | collective-permute-start | bytes 1376264 | tf_op jit(solution)/shard_map/ppermute | solution.py:73
  203.3 30.2 %collective-permute-start.28 = (bf16[64,3584]{1,0:T(8,128)(2,1)S(1)}, bf16[64,3584]{1,0:T(8,128)(2,1)S(1)}, u32[]{:S(2)}, u32[]{:S(2)}) collective-permute-start(bf16[64,3584]{1,0:T(8,128)(2,1)S(1)} %get-tuple-element.64), channel_id=1, source_target_pairs={{0,1},{1,2},{2,3},{3,4},{4,5},{5,6},{6,7},{7,0},{8,9},{9,10},{10,1... | collective-permute-start | bytes 1376264 | tf_op jit(solution)/shard_map/ppermute | solution.py:73
  205.3 21.5 %collective-permute-start.17 = (bf16[64,3584]{1,0:T(8,128)(2,1)S(1)}, bf16[64,3584]{1,0:T(8,128)(2,1)S(1)}, u32[]{:S(2)}, u32[]{:S(2)}) collective-permute-start(bf16[64,3584]{1,0:T(8,128)(2,1)S(1)} %add_convert_fusion.11), channel_id=1, source_target_pairs={{0,1},{1,2},{2,3},{3,4},{4,5},{5,6},{6,7},{7,0},{8,9},{9,10},{10,1... | collective-permute-start | bytes 1376264 | tf_op jit(solution)/shard_map/ppermute | solution.py:73
  212.2 21.3 %collective-permute-start.32 = (bf16[64,3584]{1,0:T(8,128)(2,1)S(1)}, bf16[64,3584]{1,0:T(8,128)(2,1)S(1)}, u32[]{:S(2)}, u32[]{:S(2)}) collective-permute-start(bf16[64,3584]{1,0:T(8,128)(2,1)S(1)} %add_convert_fusion.3), channel_id=1, source_target_pairs={{0,7},{1,0},{2,1},{3,2},{4,3},{5,4},{6,5},{7,6},{8,15},{9,8},{10,9... | collective-permute-start | bytes 1376264 | tf_op jit(solution)/shard_map/ppermute | solution.py:73
  227.0 15.6 %collective-permute-start.18 = (bf16[64,3584]{1,0:T(8,128)(2,1)S(1)}, bf16[64,3584]{1,0:T(8,128)(2,1)S(1)}, u32[]{:S(2)}, u32[]{:S(2)}) collective-permute-start(bf16[64,3584]{1,0:T(8,128)(2,1)S(1)} %get-tuple-element.68), channel_id=1, source_target_pairs={{0,1},{1,2},{2,3},{3,4},{4,5},{5,6},{6,7},{7,0},{8,9},{9,10},{10,1... | collective-permute-start | bytes 1376264 | tf_op jit(solution)/shard_map/ppermute | solution.py:73
  228.9 14.9 %collective-permute-start.21 = (bf16[64,3584]{1,0:T(8,128)(2,1)S(1)}, bf16[64,3584]{1,0:T(8,128)(2,1)S(1)}, u32[]{:S(2)}, u32[]{:S(2)}) collective-permute-start(bf16[64,3584]{1,0:T(8,128)(2,1)S(1)} %get-tuple-element.69), channel_id=1, source_target_pairs={{0,7},{1,0},{2,1},{3,2},{4,3},{5,4},{6,5},{7,6},{8,15},{9,8},{10,9... | collective-permute-start | bytes 1376264 | tf_op jit(solution)/shard_map/ppermute | solution.py:73
  233.7 18.7 %collective-permute-start.29 = (bf16[64,3584]{1,0:T(8,128)(2,1)S(1)}, bf16[64,3584]{1,0:T(8,128)(2,1)S(1)}, u32[]{:S(2)}, u32[]{:S(2)}) collective-permute-start(bf16[64,3584]{1,0:T(8,128)(2,1)S(1)} %get-tuple-element.62), channel_id=1, source_target_pairs={{0,1},{1,2},{2,3},{3,4},{4,5},{5,6},{6,7},{7,0},{8,9},{9,10},{10,1... | collective-permute-start | bytes 1376264 | tf_op jit(solution)/shard_map/ppermute | solution.py:73
  235.6 18.0 %collective-permute-start.33 = (bf16[64,3584]{1,0:T(8,128)(2,1)S(1)}, bf16[64,3584]{1,0:T(8,128)(2,1)S(1)}, u32[]{:S(2)}, u32[]{:S(2)}) collective-permute-start(bf16[64,3584]{1,0:T(8,128)(2,1)S(1)} %get-tuple-element.63), channel_id=1, source_target_pairs={{0,7},{1,0},{2,1},{3,2},{4,3},{5,4},{6,5},{7,6},{8,15},{9,8},{10,9... | collective-permute-start | bytes 1376264 | tf_op jit(solution)/shard_map/ppermute | solution.py:73
  244.0 18.2 %collective-permute-start.19 = (bf16[64,3584]{1,0:T(8,128)(2,1)S(1)}, bf16[64,3584]{1,0:T(8,128)(2,1)S(1)}, u32[]{:S(2)}, u32[]{:S(2)}) collective-permute-start(bf16[64,3584]{1,0:T(8,128)(2,1)S(1)} %get-tuple-element.66), channel_id=1, source_target_pairs={{0,1},{1,2},{2,3},{3,4},{4,5},{5,6},{6,7},{7,0},{8,9},{9,10},{10,1... | collective-permute-start | bytes 1376264 | tf_op jit(solution)/shard_map/ppermute | solution.py:73
  245.9 17.5 %collective-permute-start.22 = (bf16[64,3584]{1,0:T(8,128)(2,1)S(1)}, bf16[64,3584]{1,0:T(8,128)(2,1)S(1)}, u32[]{:S(2)}, u32[]{:S(2)}) collective-permute-start(bf16[64,3584]{1,0:T(8,128)(2,1)S(1)} %get-tuple-element.67), channel_id=1, source_target_pairs={{0,7},{1,0},{2,1},{3,2},{4,3},{5,4},{6,5},{7,6},{8,15},{9,8},{10,9... | collective-permute-start | bytes 1376264 | tf_op jit(solution)/shard_map/ppermute | solution.py:73
  253.8 17.4 %collective-permute-start.30 = (bf16[64,3584]{1,0:T(8,128)(2,1)S(1)}, bf16[64,3584]{1,0:T(8,128)(2,1)S(1)}, u32[]{:S(2)}, u32[]{:S(2)}) collective-permute-start(bf16[64,3584]{1,0:T(8,128)(2,1)S(1)} %get-tuple-element.60), channel_id=1, source_target_pairs={{0,1},{1,2},{2,3},{3,4},{4,5},{5,6},{6,7},{7,0},{8,9},{9,10},{10,1... | collective-permute-start | bytes 1376264 | tf_op jit(solution)/shard_map/ppermute | solution.py:73
  255.7 17.2 %collective-permute-start.34 = (bf16[64,3584]{1,0:T(8,128)(2,1)S(1)}, bf16[64,3584]{1,0:T(8,128)(2,1)S(1)}, u32[]{:S(2)}, u32[]{:S(2)}) collective-permute-start(bf16[64,3584]{1,0:T(8,128)(2,1)S(1)} %get-tuple-element.61), channel_id=1, source_target_pairs={{0,7},{1,0},{2,1},{3,2},{4,3},{5,4},{6,5},{7,6},{8,15},{9,8},{10,9... | collective-permute-start | bytes 1376264 | tf_op jit(solution)/shard_map/ppermute | solution.py:73
  263.7 15.6 %collective-permute-start.23 = (bf16[64,3584]{1,0:T(8,128)(2,1)S(1)}, bf16[64,3584]{1,0:T(8,128)(2,1)S(1)}, u32[]{:S(2)}, u32[]{:S(2)}) collective-permute-start(bf16[64,3584]{1,0:T(8,128)(2,1)S(1)} %add_convert_fusion.6), channel_id=1, source_target_pairs={{0,0},{16,32},{32,16},{48,48},{1,1},{17,33},{33,17},{49,49},{2,2},... | collective-permute-start | bytes 1376264 | tf_op jit(solution)/shard_map/ppermute | solution.py:20
  273.2 15.9 %collective-permute-start.35 = (bf16[64,3584]{1,0:T(8,128)(2,1)S(1)}, bf16[64,3584]{1,0:T(8,128)(2,1)S(1)}, u32[]{:S(2)}, u32[]{:S(2)}) collective-permute-start(bf16[64,3584]{1,0:T(8,128)(2,1)S(1)} %add_convert_fusion), channel_id=1, source_target_pairs={{0,0},{16,32},{32,16},{48,48},{1,1},{17,33},{33,17},{49,49},{2,2},... | collective-permute-start | bytes 1376264 | tf_op jit(solution)/shard_map/ppermute | solution.py:20
Sparse Core Ops, SparseCore 0:
  45.1 85.8 all-gather.1

commit v3 on v2

--- a/solution.py
+++ b/solution.py
@@ -162,17 +162,19 @@
     info = swap(jnp.pad(info, ((0, 0), (0, INFO - info.shape[1]))))
     columns = swap(jnp.pad(router[0].T, ((0, 16 - EXPERTS), (0, 0))))
     after = lax.optimization_barrier
-    x, q, info, columns, next_gate, next_up, next_down, kept_pre = after(
-        (x, q, info, columns, w_gate[0], w_up[0], w_down[0], saved_pre[:, 0])
+    a0 = swap(w_gate[0])
+    x, q, info, columns, a0, next_up, next_down, kept_pre = after(
+        (x, q, info, columns, a0, w_up[0], w_down[0], saved_pre[:, 0])
     )
     gathered = lax.all_gather(jnp.concatenate([x, q, info], axis=1), "y", axis=0, tiled=True)
-    a0 = swap(next_gate)
-    a0, next_up = after((a0, next_up))
     a1, a2, b0 = other_plane(a0), other_core(a0), swap(next_up)
     a1, b0, next_down = after((a1, b0, next_down))
     a3, b1, b2, c0 = other_core(a1), other_plane(b0), other_core(b0), swap(next_down)
-    b1, c0, wg = after((b1, c0, jnp.concatenate([a0, a1, a2, a3], axis=1)))
+    b1, c0, wg, kept_pre = after(
+        (b1, c0, jnp.concatenate([a0, a1, a2, a3], axis=1), kept_pre)
+    )
     b3, c1, c2 = other_core(b1), other_plane(c0), other_core(c0)
+    saved = [saved_of_lane(kept_pre, number) for number in range(EXPERTS)]
 
     gathered = after((gathered, c0))[0]
     wu = jnp.concatenate([b0, b1, b2, b3], axis=1)
@@ -211,13 +213,11 @@
     fgates = chosen / jnp.sum(chosen, axis=1, keepdims=True)
     fweight = side_by_side(per_block(froutes, fgates))
     gpre = jnp.dot(rows, wg, preferred_element_type=jnp.float32)
+    c1, gpre = after((c1, gpre))
     upre = jnp.dot(rows, wu, preferred_element_type=jnp.float32)
     hidden = (jax.nn.silu(gpre) * upre * fweight).astype(jnp.bfloat16)
 
-    c1, hidden = after((c1, hidden))
     c3 = other_core(c1)
-    kept_pre = after((kept_pre, c3))[0]
-    saved = [saved_of_lane(kept_pre, number) for number in range(EXPERTS)]
     wd = jnp.concatenate([c0, c1, c2, c3], axis=0)
     fpart = jnp.dot(hidden, wd, preferred_element_type=jnp.float32)
     slope_gate, slope_up = slopes(
@@ -238,6 +238,8 @@
     for _ in range(4):
         for chain in ring:
             chain.step()
+        for pair in (ring[:2], ring[2:]):
+            pair[0].total, pair[1].total = after((pair[0].total, pair[1].total))
     fsum = own_block(fpart, 0) + ring[0].total + ring[1].total
     bsum = own_block(bpart, 0) + ring[2].total + ring[3].total
     fwd_out = (x.astype(jnp.float32) + fsum).astype(jnp.bfloat16)

time: 300 us -> 303 us (1.010)
  waiting for transfers between devices: 122 us -> 98.3 us
  starting transfers between devices: 113 us -> 127 us
  other arithmetic: 10 us -> 17.1 us
  local copies, waits for them, and re-layouts: 12.5 us -> 17.9 us
    ppermute x7, starting transfers between devices: 20.1 us -> 32.9 us  [swap(): return lax.ppermute(array, ('c', 'u'), [(0, 0), (1, 2), (2, 1), (3, 3)])]
    ppermute x14, waiting for transfers between devices: 29.1 us -> 16.5 us  [neighbour(): lax.ppermute(array, 'y', [(i, (i + by) % LANES) for i in range(LANES)])]
    ppermute x7, waiting for transfers between devices: 49 us -> 37.9 us  [swap(): return lax.ppermute(array, ('c', 'u'), [(0, 0), (1, 2), (2, 1), (3, 3)])]
    ppermute x3, waiting for transfers between devices: 35.3 us -> 42.9 us  [other_plane(): return lax.ppermute(array, 'v', [(0, 1), (1, 0)])]
    ppermute x2, waiting for transfers between devices: 6.63 us -> 0.01 us  [shift_and_swap(): return lax.ppermute(array, ('x', 'h', 'c', 'u'), pairs)]
    add x0 -> x6, other arithmetic: none -> 6.55 us  [step(): self.total = received + own_block(self.terms, self.by * self.left)]
    unnamed x23 -> x29, local copies, waits for them, and re-layouts: 8.94 us -> 14.3 us
    ppermute x2, starting transfers between devices: 13.9 us -> 8.56 us  [shift_and_swap(): return lax.ppermute(array, ('x', 'h', 'c', 'u'), pairs)]
  transfers between devices with their start and end apart: 37 -> 37, of which waited for: 19 -> 16; matrix products, arithmetic and copies ran while one was open for 15% -> 14% of each run, Pallas kernels for 1% -> 1%
where the time goes in v3:
time: 303 us; the launch traced here: 301 us
  starting transfers between devices  127 us (42%)
  waiting for transfers between devices  98.3 us (32%)
  matrix products  23.8 us (8%)
  local copies, waits for them, and re-layouts  17.9 us (6%)
  other arithmetic  17.1 us (6%)
  between operations  15 us (5%)
    ppermute x14, starting transfers between devices, neighbour(): lax.ppermute(array, 'y', [(i, (i + by) % LANES) for i in range(LANES)])  50.7 us
    ppermute x3, waiting for transfers between devices, other_plane(): return lax.ppermute(array, 'v', [(0, 1), (1, 0)])  42.9 us
    ppermute x7, waiting for transfers between devices, swap(): return lax.ppermute(array, ('c', 'u'), [(0, 0), (1, 2), (2, 1), (3, 3)])  37.9 us
    ppermute x7, starting transfers between devices, swap(): return lax.ppermute(array, ('c', 'u'), [(0, 0), (1, 2), (2, 1), (3, 3)])  32.9 us
    ppermute x14, waiting for transfers between devices, neighbour(): lax.ppermute(array, 'y', [(i, (i + by) % LANES) for i in range(LANES)])  16.5 us
    unnamed x29, local copies, waits for them, and re-layouts  14.3 us
    ppermute x4, starting transfers between devices, saved_of_lane(): lax.ppermute(jnp.concatenate([part[0], part[1]], axis=1), ('c', 'u', 'v')...  14 us
    ppermute x6, starting transfers between devices, other_core(): return lax.ppermute(array, 'c', [(0, 1), (1, 0)])  12.7 us
  transfers between devices with their start and end apart: 37, of which 16 were waited for; matrix products, arithmetic and copies ran while one was open for 14% of the time, Pallas kernels for 1%

profile of v3, /device:TPU:1, one launch (start us, length us, event | category | flops | bytes accessed | tf_op | source)
XLA Modules:
  0.0 300.7 jit_solution(13897119026348624890)
XLA Ops:
  7.2 7.2 %collective-permute-start.4 = (bf16[3584,128]{1,0:T(8,128)(2,1)}, bf16[3584,128]{1,0:T(8,128)(2,1)S(1)}, u32[]{:S(2)}, u32[]{:S(2)}) collective-permute-start(bf16[3584,128]{1,0:T(8,128)(2,1)} %bitcast.44), channel_id=1, source_target_pairs={{0,0},{16,32},{32,16},{48,48},{1,1},{17,33},{33,17},{49,49},{2,2},... | collective-permute-start | bytes 2752520 | tf_op jit(solution)/shard_map/ppermute | solution.py:20
  14.4 6.6 %collective-permute-start = (bf16[64,3584]{1,0:T(8,128)(2,1)}, bf16[64,3584]{1,0:T(8,128)(2,1)S(1)}, u32[]{:S(2)}, u32[]{:S(2)}) collective-permute-start(bf16[64,3584]{1,0:T(8,128)(2,1)} %param.10), channel_id=1, source_target_pairs={{0,16},{16,48},{32,64},{48,96},{64,80},{80,112},{96,128},{112,160}... | collective-permute-start | bytes 1376264 | tf_op jit(solution)/shard_map/ppermute | solution.py:31
  23.8 5.9 %collective-permute-start.3 = (bf16[16,3584]{1,0:T(8,128)(2,1)S(1)}, bf16[16,3584]{1,0:T(8,128)(2,1)S(1)}, u32[]{:S(2)}, u32[]{:S(2)}) collective-permute-start(bf16[16,3584]{1,0:T(8,128)(2,1)S(1)} %pad.9), channel_id=1, source_target_pairs={{0,0},{16,32},{32,16},{48,48},{1,1},{17,33},{33,17},{49,49},{2,2},... | collective-permute-start | bytes 344072 | tf_op jit(solution)/shard_map/ppermute | solution.py:20
  34.8 23.2 %collective-permute-done.2 = bf16[64,128]{1,0:T(8,128)(2,1)S(1)} collective-permute-done((bf16[64,128]{1,0:T(8,128)(2,1)S(1)}, bf16[64,128]{1,0:T(8,128)(2,1)S(1)}, u32[]{:S(2)}, u32[]{:S(2)}) %collective-permute-start.2) | collective-permute-done | bytes 16416 | tf_op jit(solution)/shard_map/ppermute | solution.py:20
  59.1 2.4 collective-permute-start.5
  61.5 5.6 %collective-permute-start.6 = (bf16[3584,128]{1,0:T(8,128)(2,1)}, bf16[3584,128]{1,0:T(8,128)(2,1)}, u32[]{:S(2)}, u32[]{:S(2)}) collective-permute-start(bf16[3584,128]{1,0:T(8,128)(2,1)} %bitcast.45), channel_id=1, source_target_pairs={{0,0},{16,32},{32,16},{48,48},{1,1},{17,33},{33,17},{49,49},{2,2},... | collective-permute-start | bytes 2752520 | tf_op jit(solution)/shard_map/ppermute | solution.py:20
  67.1 1.9 collective-permute-start.9
  69.0 22.2 %collective-permute-done.5 = bf16[3584,128]{1,0:T(8,128)(2,1)S(1)} collective-permute-done((bf16[3584,128]{1,0:T(8,128)(2,1)S(1)}, bf16[3584,128]{1,0:T(8,128)(2,1)S(1)}, u32[]{:S(2)}, u32[]{:S(2)}) %collective-permute-start.5) | collective-permute-done | bytes 917536 | tf_op jit(solution)/shard_map/ppermute | solution.py:35
  95.2 2.4 collective-permute-start.12
  97.6 2.8 collective-permute-start.8
  100.4 2.2 constant_dynamic-update-slice_fusion.3
  102.7 3.3 %pad_maximum_fusion = bf16[3584,512]{1,0:T(8,128)(2,1)} fusion(bf16[3584,128]{1,0:T(8,128)(2,1)} %collective-permute-done.10, bf16[3584,128]{1,0:T(8,128)(2,1)} %collective-permute-done.9, bf16[3584,128]{1,0:T(8,128)(2,1)S(1)} %collective-permute-done.5, bf16[3584,128]{1,0:T(8,128)(2,1)S(1)} %collective-permute-done.4), kind=kLoop, calls=%fused_computation.1 | loop fusion | flops 14680064 | bytes 7340032 | tf_op jit(solution)/shard_map/concatenate | solution.py:174
  106.0 20.7 %collective-permute-done.7 = bf16[3584,128]{1,0:T(8,128)(2,1)S(1)} collective-permute-done((bf16[3584,128]{1,0:T(8,128)(2,1)}, bf16[3584,128]{1,0:T(8,128)(2,1)S(1)}, u32[]{:S(2)}, u32[]{:S(2)}) %collective-permute-start.7) | collective-permute-done | bytes 917536 | tf_op jit(solution)/shard_map/ppermute | solution.py:35
  126.7 3.9 %collective-permute-start.11 = (bf16[128,3584]{1,0:T(8,128)(2,1)}, bf16[128,3584]{1,0:T(8,128)(2,1)S(1)}, u32[]{:S(2)}, u32[]{:S(2)}) collective-permute-start(bf16[128,3584]{1,0:T(8,128)(2,1)} %collective-permute-done.8), channel_id=1, source_target_pairs={{0,8},{8,0},{1,9},{9,1},{2,10},{10,2},{3,11},{11,3},{4,12},{12,4},... | collective-permute-start | bytes 2752520 | tf_op jit(solution)/shard_map/ppermute | solution.py:35
  130.6 1.9 collective-permute-start.14
  132.5 2.4 collective-permute-start.13
  135.0 2.4 collective-permute-start.24
  137.5 2.2 constant_dynamic-update-slice_fusion.7
  140.7 4.3 %collective-permute-start.25 = (bf16[272,256]{1,0:T(8,128)(2,1)S(1)}, bf16[272,256]{1,0:T(8,128)(2,1)S(1)}, u32[]{:S(2)}, u32[]{:S(2)}) collective-permute-start(bf16[272,256]{1,0:T(8,128)(2,1)S(1)} %pad_maximum_fusion.3), channel_id=1, source_target_pairs={{0,8},{8,0},{16,40},{24,32},{32,24},{40,16},{48,56},{56,48},{1,9},... | collective-permute-start | bytes 417800 | tf_op jit(solution)/shard_map/ppermute | solution.py:51
  151.1 6.4 %fusion.6 = f32[512,512]{1,0:T(8,128)} fusion(bf16[3584,512]{1,0:T(8,128)(2,1)} %pad_maximum_fusion, bf16[512,7296]{1,0:T(8,128)(2,1)} %all-gather.2.cloned.1.call-done.info_ref), kind=kOutput, calls=%fused_computation.8 | convolution fusion | flops 1879048192 | bytes 8388608 | tf_op jit(solution)/shard_map/dot_general | solution.py:215
  157.5 5.4 %collective-permute-start.27 = (bf16[272,256]{1,0:T(8,128)(2,1)S(1)}, bf16[272,256]{1,0:T(8,128)(2,1)S(1)}, u32[]{:S(2)}, u32[]{:S(2)}) collective-permute-start(bf16[272,256]{1,0:T(8,128)(2,1)S(1)} %pad_maximum_fusion.5), channel_id=1, source_target_pairs={{0,40},{8,32},{16,8},{24,0},{32,56},{40,48},{48,24},{56,16},{1,41}... | collective-permute-start | bytes 417800 | tf_op jit(solution)/shard_map/ppermute | solution.py:51
  166.5 5.7 %fusion.20 = bf16[512,512]{1,0:T(8,128)(2,1)S(1)} fusion(f32[512,128]{1,0:T(8,128)S(1)} %broadcast_in_dim.54, f32[512,128]{1,0:T(8,128)S(1)} %broadcast_in_dim.53, f32[512,128]{1,0:T(8,128)S(1)} %broadcast_in_dim.52, f32[512,128]{1,0:T(8,128)S(1)} %broadcast_in_dim.51, f32[512,512]{1,0:T(8,128)} %fusion.6, ...), kind=kOutput, calls=%fused_computation.15 | convolution fusion | flops 1881669632 | bytes 9961472 | tf_op jit(solution)/shard_map/dot_general | solution.py:217
  172.2 2.1 collective-permute-start.15
  177.8 2.1 fusion.27
  179.9 2.1 multiply_convert_fusion
  182.9 4.3 %fusion.28 = f32[512,3584]{1,0:T(8,128)S(1)} fusion(bf16[512,512]{1,0:T(8,128)(2,1)S(1)} %get-tuple-element.71, bf16[3584,512]{1,0:T(8,128)(2,1)} %constant_dynamic-update-slice_fusion), kind=kOutput, calls=%fused_computation.83 | convolution fusion | flops 1879048192 | bytes 11534336 | tf_op jit(solution)/shard_map/dot_general | solution.py:236
  187.2 2.1 convolution_add_fusion
  189.3 3.0 copy-done
  192.4 1.9 collective-permute-start.28
  194.4 4.6 %collective-permute-start.29 = (bf16[64,3584]{1,0:T(8,128)(2,1)S(1)}, bf16[64,3584]{1,0:T(8,128)(2,1)}, u32[]{:S(2)}, u32[]{:S(2)}) collective-permute-start(bf16[64,3584]{1,0:T(8,128)(2,1)S(1)} %get-tuple-element.92), channel_id=1, source_target_pairs={{0,7},{1,0},{2,1},{3,2},{4,3},{5,4},{6,5},{7,6},{8,15},{9,8},{10,9... | collective-permute-start | bytes 1376264 | tf_op jit(solution)/shard_map/ppermute | solution.py:73
  199.0 2.3 collective-permute-start.16
  201.4 4.4 %collective-permute-start.17 = (bf16[64,3584]{1,0:T(8,128)(2,1)S(1)}, bf16[64,3584]{1,0:T(8,128)(2,1)S(1)}, u32[]{:S(2)}, u32[]{:S(2)}) collective-permute-start(bf16[64,3584]{1,0:T(8,128)(2,1)S(1)} %get-tuple-element.98), channel_id=1, source_target_pairs={{0,7},{1,0},{2,1},{3,2},{4,3},{5,4},{6,5},{7,6},{8,15},{9,8},{10,9... | collective-permute-start | bytes 1376264 | tf_op jit(solution)/shard_map/ppermute | solution.py:73
  209.7 3.8 %collective-permute-start.30 = (bf16[64,3584]{1,0:T(8,128)(2,1)S(1)}, bf16[64,3584]{1,0:T(8,128)(2,1)S(1)}, u32[]{:S(2)}, u32[]{:S(2)}) collective-permute-start(bf16[64,3584]{1,0:T(8,128)(2,1)S(1)} %get-tuple-element.72), channel_id=1, source_target_pairs={{0,1},{1,2},{2,3},{3,4},{4,5},{5,6},{6,7},{7,0},{8,9},{9,10},{10,1... | collective-permute-start | bytes 1376264 | tf_op jit(solution)/shard_map/ppermute | solution.py:73
  213.6 3.5 %collective-permute-start.31 = (bf16[64,3584]{1,0:T(8,128)(2,1)S(1)}, bf16[64,3584]{1,0:T(8,128)(2,1)S(1)}, u32[]{:S(2)}, u32[]{:S(2)}) collective-permute-start(bf16[64,3584]{1,0:T(8,128)(2,1)S(1)} %get-tuple-element.73), channel_id=1, source_target_pairs={{0,7},{1,0},{2,1},{3,2},{4,3},{5,4},{6,5},{7,6},{8,15},{9,8},{10,9... | collective-permute-start | bytes 1376264 | tf_op jit(solution)/shard_map/ppermute | solution.py:73
  219.5 3.7 %collective-permute-start.18 = (bf16[64,3584]{1,0:T(8,128)(2,1)S(1)}, bf16[64,3584]{1,0:T(8,128)(2,1)S(1)}, u32[]{:S(2)}, u32[]{:S(2)}) collective-permute-start(bf16[64,3584]{1,0:T(8,128)(2,1)S(1)} %get-tuple-element.58), channel_id=1, source_target_pairs={{0,1},{1,2},{2,3},{3,4},{4,5},{5,6},{6,7},{7,0},{8,9},{9,10},{10,1... | collective-permute-start | bytes 1376264 | tf_op jit(solution)/shard_map/ppermute | solution.py:73
  223.2 3.5 %collective-permute-start.19 = (bf16[64,3584]{1,0:T(8,128)(2,1)S(1)}, bf16[64,3584]{1,0:T(8,128)(2,1)S(1)}, u32[]{:S(2)}, u32[]{:S(2)}) collective-permute-start(bf16[64,3584]{1,0:T(8,128)(2,1)S(1)} %get-tuple-element.59), channel_id=1, source_target_pairs={{0,7},{1,0},{2,1},{3,2},{4,3},{5,4},{6,5},{7,6},{8,15},{9,8},{10,9... | collective-permute-start | bytes 1376264 | tf_op jit(solution)/shard_map/ppermute | solution.py:73
  227.2 5.3 %collective-permute-start.33 = (bf16[64,3584]{1,0:T(8,128)(2,1)S(1)}, bf16[64,3584]{1,0:T(8,128)(2,1)S(1)}, u32[]{:S(2)}, u32[]{:S(2)}) collective-permute-start(bf16[64,3584]{1,0:T(8,128)(2,1)S(1)} %get-tuple-element.75), channel_id=1, source_target_pairs={{0,7},{1,0},{2,1},{3,2},{4,3},{5,4},{6,5},{7,6},{8,15},{9,8},{10,9... | collective-permute-start | bytes 1376264 | tf_op jit(solution)/shard_map/ppermute | solution.py:73
  232.5 1.9 collective-permute-start.32
  238.6 5.3 %collective-permute-start.21 = (bf16[64,3584]{1,0:T(8,128)(2,1)S(1)}, bf16[64,3584]{1,0:T(8,128)(2,1)S(1)}, u32[]{:S(2)}, u32[]{:S(2)}) collective-permute-start(bf16[64,3584]{1,0:T(8,128)(2,1)S(1)} %get-tuple-element.61), channel_id=1, source_target_pairs={{0,7},{1,0},{2,1},{3,2},{4,3},{5,4},{6,5},{7,6},{8,15},{9,8},{10,9... | collective-permute-start | bytes 1376264 | tf_op jit(solution)/shard_map/ppermute | solution.py:73
  244.0 1.9 collective-permute-start.20
  247.0 5.3 %collective-permute-start.34 = (bf16[64,3584]{1,0:T(8,128)(2,1)S(1)}, bf16[64,3584]{1,0:T(8,128)(2,1)S(1)}, u32[]{:S(2)}, u32[]{:S(2)}) collective-permute-start(bf16[64,3584]{1,0:T(8,128)(2,1)S(1)} %dynamic-slice_add_fusion), channel_id=1, source_target_pairs={{0,7},{1,0},{2,1},{3,2},{4,3},{5,4},{6,5},{7,6},{8,15},{9,8},{10,9... | collective-permute-start | bytes 1376264 | tf_op jit(solution)/shard_map/ppermute | solution.py:73
  252.3 2.6 collective-permute-done.20
  256.7 3.0 %collective-permute-start.22 = (bf16[64,3584]{1,0:T(8,128)(2,1)S(1)}, bf16[64,3584]{1,0:T(8,128)(2,1)S(1)}, u32[]{:S(2)}, u32[]{:S(2)}) collective-permute-start(bf16[64,3584]{1,0:T(8,128)(2,1)S(1)} %dynamic-slice_add_fusion.5), channel_id=1, source_target_pairs={{0,1},{1,2},{2,3},{3,4},{4,5},{5,6},{6,7},{7,0},{8,9},{9,10},{10,1... | collective-permute-start | bytes 1376264 | tf_op jit(solution)/shard_map/ppermute | solution.py:73
  259.7 6.7 %collective-permute-done.34 = bf16[64,3584]{1,0:T(8,128)(2,1)S(1)} collective-permute-done((bf16[64,3584]{1,0:T(8,128)(2,1)S(1)}, bf16[64,3584]{1,0:T(8,128)(2,1)S(1)}, u32[]{:S(2)}, u32[]{:S(2)}) %collective-permute-start.34) | collective-permute-done | bytes 458784 | tf_op jit(solution)/shard_map/ppermute | solution.py:73
  266.8 4.8 %collective-permute-start.35 = (bf16[64,3584]{1,0:T(8,128)(2,1)S(1)}, bf16[64,3584]{1,0:T(8,128)(2,1)S(1)}, u32[]{:S(2)}, u32[]{:S(2)}) collective-permute-start(bf16[64,3584]{1,0:T(8,128)(2,1)S(1)} %add_convert_fusion), channel_id=1, source_target_pairs={{0,0},{16,32},{32,16},{48,48},{1,1},{17,33},{33,17},{49,49},{2,2},... | collective-permute-start | bytes 1376264 | tf_op jit(solution)/shard_map/ppermute | solution.py:20
  273.0 4.6 %collective-permute-start.23 = (bf16[64,3584]{1,0:T(8,128)(2,1)S(1)}, bf16[64,3584]{1,0:T(8,128)(2,1)S(1)}, u32[]{:S(2)}, u32[]{:S(2)}) collective-permute-start(bf16[64,3584]{1,0:T(8,128)(2,1)S(1)} %add_convert_fusion.1), channel_id=1, source_target_pairs={{0,0},{16,32},{32,16},{48,48},{1,1},{17,33},{33,17},{49,49},{2,2},... | collective-permute-start | bytes 1376264 | tf_op jit(solution)/shard_map/ppermute | solution.py:20
  277.6 9.7 %collective-permute-done.35 = bf16[64,3584]{1,0:T(8,128)(2,1)S(1)} collective-permute-done((bf16[64,3584]{1,0:T(8,128)(2,1)S(1)}, bf16[64,3584]{1,0:T(8,128)(2,1)S(1)}, u32[]{:S(2)}, u32[]{:S(2)}) %collective-permute-start.35) | collective-permute-done | bytes 458784 | tf_op jit(solution)/shard_map/ppermute | solution.py:20
  287.4 4.9 %collective-permute-done.23 = bf16[64,3584]{1,0:T(8,128)(2,1)S(1)} collective-permute-done((bf16[64,3584]{1,0:T(8,128)(2,1)S(1)}, bf16[64,3584]{1,0:T(8,128)(2,1)S(1)}, u32[]{:S(2)}, u32[]{:S(2)}) %collective-permute-start.23) | collective-permute-done | bytes 458784 | tf_op jit(solution)/shard_map/ppermute | solution.py:20
  (111 shorter events, 44.7 us)
Async XLA Ops:
  7.2 142.8 %all-gather.2.cloned.1.call-start = ((), (), s32[]{:S(2)}) async-start(), calls=%async_computation | async-start | bytes 8404992 | tf_op jit(solution)/shard_map/all_gather | solution.py:169
  7.2 50.8 %collective-permute-start.4 = (bf16[3584,128]{1,0:T(8,128)(2,1)}, bf16[3584,128]{1,0:T(8,128)(2,1)S(1)}, u32[]{:S(2)}, u32[]{:S(2)}) collective-permute-start(bf16[3584,128]{1,0:T(8,128)(2,1)} %bitcast.44), channel_id=1, source_target_pairs={{0,0},{16,32},{32,16},{48,48},{1,1},{17,33},{33,17},{49,49},{2,2},... | collective-permute-start | bytes 2752520 | tf_op jit(solution)/shard_map/ppermute | solution.py:20
  14.4 43.6 %collective-permute-start = (bf16[64,3584]{1,0:T(8,128)(2,1)}, bf16[64,3584]{1,0:T(8,128)(2,1)S(1)}, u32[]{:S(2)}, u32[]{:S(2)}) collective-permute-start(bf16[64,3584]{1,0:T(8,128)(2,1)} %param.10), channel_id=1, source_target_pairs={{0,16},{16,48},{32,64},{48,96},{64,80},{80,112},{96,128},{112,160}... | collective-permute-start | bytes 1376264 | tf_op jit(solution)/shard_map/ppermute | solution.py:31
  21.1 36.9 %collective-permute-start.1 = (bf16[64,3584]{1,0:T(8,128)(2,1)}, bf16[64,3584]{1,0:T(8,128)(2,1)S(1)}, u32[]{:S(2)}, u32[]{:S(2)}) collective-permute-start(bf16[64,3584]{1,0:T(8,128)(2,1)} %param.13), channel_id=1, source_target_pairs={{0,464},{16,496},{32,0},{48,32},{64,16},{80,48},{96,64},{112,96},{... | collective-permute-start | bytes 1376264 | tf_op jit(solution)/shard_map/ppermute | solution.py:31
  23.8 34.2 %collective-permute-start.3 = (bf16[16,3584]{1,0:T(8,128)(2,1)S(1)}, bf16[16,3584]{1,0:T(8,128)(2,1)S(1)}, u32[]{:S(2)}, u32[]{:S(2)}) collective-permute-start(bf16[16,3584]{1,0:T(8,128)(2,1)S(1)} %pad.9), channel_id=1, source_target_pairs={{0,0},{16,32},{32,16},{48,48},{1,1},{17,33},{33,17},{49,49},{2,2},... | collective-permute-start | bytes 344072 | tf_op jit(solution)/shard_map/ppermute | solution.py:20
  32.8 25.1 %collective-permute-start.2 = (bf16[64,128]{1,0:T(8,128)(2,1)S(1)}, bf16[64,128]{1,0:T(8,128)(2,1)S(1)}, u32[]{:S(2)}, u32[]{:S(2)}) collective-permute-start(bf16[64,128]{1,0:T(8,128)(2,1)S(1)} %pad.8), channel_id=1, source_target_pairs={{0,0},{16,32},{32,16},{48,48},{1,1},{17,33},{33,17},{49,49},{2,2},... | collective-permute-start | bytes 49160 | tf_op jit(solution)/shard_map/ppermute | solution.py:20
  59.1 32.2 %collective-permute-start.5 = (bf16[3584,128]{1,0:T(8,128)(2,1)S(1)}, bf16[3584,128]{1,0:T(8,128)(2,1)S(1)}, u32[]{:S(2)}, u32[]{:S(2)}) collective-permute-start(bf16[3584,128]{1,0:T(8,128)(2,1)S(1)} %collective-permute-done.4), channel_id=1, source_target_pairs={{0,8},{8,0},{1,9},{9,1},{2,10},{10,2},{3,11},{11,3},{4,12},{12,4},... | collective-permute-start | bytes 2752520 | tf_op jit(solution)/shard_map/ppermute | solution.py:35
  61.5 29.8 %collective-permute-start.6 = (bf16[3584,128]{1,0:T(8,128)(2,1)}, bf16[3584,128]{1,0:T(8,128)(2,1)}, u32[]{:S(2)}, u32[]{:S(2)}) collective-permute-start(bf16[3584,128]{1,0:T(8,128)(2,1)} %bitcast.45), channel_id=1, source_target_pairs={{0,0},{16,32},{32,16},{48,48},{1,1},{17,33},{33,17},{49,49},{2,2},... | collective-permute-start | bytes 2752520 | tf_op jit(solution)/shard_map/ppermute | solution.py:20
  67.1 35.6 %collective-permute-start.9 = (bf16[3584,128]{1,0:T(8,128)(2,1)S(1)}, bf16[3584,128]{1,0:T(8,128)(2,1)}, u32[]{:S(2)}, u32[]{:S(2)}) collective-permute-start(bf16[3584,128]{1,0:T(8,128)(2,1)S(1)} %collective-permute-done.4), channel_id=1, source_target_pairs={{0,32},{32,0},{1,33},{33,1},{2,34},{34,2},{3,35},{35,3},{4,36},{36... | collective-permute-start | bytes 2752520 | tf_op jit(solution)/shard_map/ppermute | solution.py:39
  91.2 11.4 %collective-permute-start.10 = (bf16[3584,128]{1,0:T(8,128)(2,1)S(1)}, bf16[3584,128]{1,0:T(8,128)(2,1)}, u32[]{:S(2)}, u32[]{:S(2)}) collective-permute-start(bf16[3584,128]{1,0:T(8,128)(2,1)S(1)} %collective-permute-done.5), channel_id=1, source_target_pairs={{0,32},{32,0},{1,33},{33,1},{2,34},{34,2},{3,35},{35,3},{4,36},{36... | collective-permute-start | bytes 2752520 | tf_op jit(solution)/shard_map/ppermute | solution.py:39
  93.3 33.5 %collective-permute-start.7 = (bf16[3584,128]{1,0:T(8,128)(2,1)}, bf16[3584,128]{1,0:T(8,128)(2,1)S(1)}, u32[]{:S(2)}, u32[]{:S(2)}) collective-permute-start(bf16[3584,128]{1,0:T(8,128)(2,1)} %collective-permute-done.6), channel_id=1, source_target_pairs={{0,8},{8,0},{1,9},{9,1},{2,10},{10,2},{3,11},{11,3},{4,12},{12,4},... | collective-permute-start | bytes 2752520 | tf_op jit(solution)/shard_map/ppermute | solution.py:35
  95.2 45.6 %collective-permute-start.12 = (bf16[3584,128]{1,0:T(8,128)(2,1)}, bf16[3584,128]{1,0:T(8,128)(2,1)S(1)}, u32[]{:S(2)}, u32[]{:S(2)}) collective-permute-start(bf16[3584,128]{1,0:T(8,128)(2,1)} %collective-permute-done.6), channel_id=1, source_target_pairs={{0,32},{32,0},{1,33},{33,1},{2,34},{34,2},{3,35},{35,3},{4,36},{36... | collective-permute-start | bytes 2752520 | tf_op jit(solution)/shard_map/ppermute | solution.py:39
  97.6 29.1 %collective-permute-start.8 = (bf16[128,3584]{1,0:T(8,128)(2,1)}, bf16[128,3584]{1,0:T(8,128)(2,1)}, u32[]{:S(2)}, u32[]{:S(2)}) collective-permute-start(bf16[128,3584]{1,0:T(8,128)(2,1)} %bitcast.46), channel_id=1, source_target_pairs={{0,0},{16,32},{32,16},{48,48},{1,1},{17,33},{33,17},{49,49},{2,2},... | collective-permute-start | bytes 2752520 | tf_op jit(solution)/shard_map/ppermute | solution.py:20
  102.6 32.3 %copy-start.5 = (bf16[2,1,1088,128]{3,2,1,0:T(8,128)(2,1)S(1)}, bf16[2,1,1088,128]{3,2,1,0:T(8,128)(2,1)}, u32[]{:S(2)}) copy-start(bf16[2,1,1088,128]{3,2,1,0:T(8,128)(2,1)} %param.19) | copy-start | bytes 1671172
  126.7 30.8 %collective-permute-start.11 = (bf16[128,3584]{1,0:T(8,128)(2,1)}, bf16[128,3584]{1,0:T(8,128)(2,1)S(1)}, u32[]{:S(2)}, u32[]{:S(2)}) collective-permute-start(bf16[128,3584]{1,0:T(8,128)(2,1)} %collective-permute-done.8), channel_id=1, source_target_pairs={{0,8},{8,0},{1,9},{9,1},{2,10},{10,2},{3,11},{11,3},{4,12},{12,4},... | collective-permute-start | bytes 2752520 | tf_op jit(solution)/shard_map/ppermute | solution.py:35
  130.6 45.9 %collective-permute-start.14 = (bf16[128,3584]{1,0:T(8,128)(2,1)}, bf16[128,3584]{1,0:T(8,128)(2,1)}, u32[]{:S(2)}, u32[]{:S(2)}) collective-permute-start(bf16[128,3584]{1,0:T(8,128)(2,1)} %collective-permute-done.8), channel_id=1, source_target_pairs={{0,32},{32,0},{1,33},{33,1},{2,34},{34,2},{3,35},{35,3},{4,36},{36... | collective-permute-start | bytes 2752520 | tf_op jit(solution)/shard_map/ppermute | solution.py:39
  132.5 13.6 %collective-permute-start.13 = (bf16[3584,128]{1,0:T(8,128)(2,1)S(1)}, bf16[3584,128]{1,0:T(8,128)(2,1)S(1)}, u32[]{:S(2)}, u32[]{:S(2)}) collective-permute-start(bf16[3584,128]{1,0:T(8,128)(2,1)S(1)} %collective-permute-done.7), channel_id=1, source_target_pairs={{0,32},{32,0},{1,33},{33,1},{2,34},{34,2},{3,35},{35,3},{4,36},{36... | collective-permute-start | bytes 2752520 | tf_op jit(solution)/shard_map/ppermute | solution.py:39
  135.0 37.1 %collective-permute-start.24 = (bf16[272,256]{1,0:T(8,128)(2,1)S(1)}, bf16[272,256]{1,0:T(8,128)(2,1)S(1)}, u32[]{:S(2)}, u32[]{:S(2)}) collective-permute-start(bf16[272,256]{1,0:T(8,128)(2,1)S(1)} %pad_maximum_fusion.2), channel_id=1, source_target_pairs={{0,0},{8,8},{16,32},{24,40},{32,16},{40,24},{48,48},{56,56},{1,1},... | collective-permute-start | bytes 417800 | tf_op jit(solution)/shard_map/ppermute | solution.py:51
  140.7 33.5 %collective-permute-start.25 = (bf16[272,256]{1,0:T(8,128)(2,1)S(1)}, bf16[272,256]{1,0:T(8,128)(2,1)S(1)}, u32[]{:S(2)}, u32[]{:S(2)}) collective-permute-start(bf16[272,256]{1,0:T(8,128)(2,1)S(1)} %pad_maximum_fusion.3), channel_id=1, source_target_pairs={{0,8},{8,0},{16,40},{24,32},{32,24},{40,16},{48,56},{56,48},{1,9},... | collective-permute-start | bytes 417800 | tf_op jit(solution)/shard_map/ppermute | solution.py:51
  146.1 28.2 %collective-permute-start.26 = (bf16[272,256]{1,0:T(8,128)(2,1)S(1)}, bf16[272,256]{1,0:T(8,128)(2,1)S(1)}, u32[]{:S(2)}, u32[]{:S(2)}) collective-permute-start(bf16[272,256]{1,0:T(8,128)(2,1)S(1)} %pad_maximum_fusion.4), channel_id=1, source_target_pairs={{0,32},{8,40},{16,0},{24,8},{32,48},{40,56},{48,16},{56,24},{1,33}... | collective-permute-start | bytes 417800 | tf_op jit(solution)/shard_map/ppermute | solution.py:51
  150.0 13.3 %slice-start = ((s8[7471104]{0:T(1024)(128)(4,1)}), s8[4194304]{0:T(1024)(128)(4,1)S(1)}, s32[]{:S(2)}) async-start(s8[7471104]{0:T(1024)(128)(4,1)} %bitcast.36), calls=%async_computation.1 | async-start | bytes 8388608
  151.1 12.2 %slice-start.1 = ((s8[7471104]{0:T(1024)(128)(4,1)}), s8[3276800]{0:T(1024)(128)(4,1)S(1)}, s32[]{:S(2)}) async-start(s8[7471104]{0:T(1024)(128)(4,1)} %bitcast.36), calls=%async_computation.2 | async-start | bytes 6553600
  157.5 16.8 %collective-permute-start.27 = (bf16[272,256]{1,0:T(8,128)(2,1)S(1)}, bf16[272,256]{1,0:T(8,128)(2,1)S(1)}, u32[]{:S(2)}, u32[]{:S(2)}) collective-permute-start(bf16[272,256]{1,0:T(8,128)(2,1)S(1)} %pad_maximum_fusion.5), channel_id=1, source_target_pairs={{0,40},{8,32},{16,8},{24,0},{32,56},{40,48},{48,24},{56,16},{1,41}... | collective-permute-start | bytes 417800 | tf_op jit(solution)/shard_map/ppermute | solution.py:51
  166.3 8.0 %slice-start.2 = ((s8[7471104]{0:T(1024)(128)(4,1)}), s8[4194304]{0:T(1024)(128)(4,1)S(1)}, s32[]{:S(2)}) async-start(s8[7471104]{0:T(1024)(128)(4,1)} %bitcast.38), calls=%async_computation.3 | async-start | bytes 8388608
  166.4 7.9 %slice-start.3 = ((s8[7471104]{0:T(1024)(128)(4,1)}), s8[3276800]{0:T(1024)(128)(4,1)S(1)}, s32[]{:S(2)}) async-start(s8[7471104]{0:T(1024)(128)(4,1)} %bitcast.38), calls=%async_computation.4 | async-start | bytes 6553600
  172.2 5.5 %collective-permute-start.15 = (bf16[128,3584]{1,0:T(8,128)(2,1)S(1)}, bf16[128,3584]{1,0:T(8,128)(2,1)S(1)}, u32[]{:S(2)}, u32[]{:S(2)}) collective-permute-start(bf16[128,3584]{1,0:T(8,128)(2,1)S(1)} %collective-permute-done.11), channel_id=1, source_target_pairs={{0,32},{32,0},{1,33},{33,1},{2,34},{34,2},{3,35},{35,3},{4,36},{36... | collective-permute-start | bytes 2752520 | tf_op jit(solution)/shard_map/ppermute | solution.py:39
  174.3 2.0 copy-start.4
  179.9 2.9 copy-start.2
  182.9 4.3 %copy-start.3 = (bf16[3584,512]{1,0:T(8,128)(2,1)S(1)}, bf16[3584,512]{1,0:T(8,128)(2,1)}, u32[]{:S(2)}) copy-start(bf16[3584,512]{1,0:T(8,128)(2,1)} %pad_maximum_fusion) | copy-start | bytes 11010052
  189.3 3.0 copy-start
  192.4 14.7 %collective-permute-start.28 = (bf16[64,3584]{1,0:T(8,128)(2,1)S(1)}, bf16[64,3584]{1,0:T(8,128)(2,1)S(1)}, u32[]{:S(2)}, u32[]{:S(2)}) collective-permute-start(bf16[64,3584]{1,0:T(8,128)(2,1)S(1)} %get-tuple-element.93), channel_id=1, source_target_pairs={{0,1},{1,2},{2,3},{3,4},{4,5},{5,6},{6,7},{7,0},{8,9},{9,10},{10,1... | collective-permute-start | bytes 1376264 | tf_op jit(solution)/shard_map/ppermute | solution.py:73
  194.4 13.6 %collective-permute-start.29 = (bf16[64,3584]{1,0:T(8,128)(2,1)S(1)}, bf16[64,3584]{1,0:T(8,128)(2,1)}, u32[]{:S(2)}, u32[]{:S(2)}) collective-permute-start(bf16[64,3584]{1,0:T(8,128)(2,1)S(1)} %get-tuple-element.92), channel_id=1, source_target_pairs={{0,7},{1,0},{2,1},{3,2},{4,3},{5,4},{6,5},{7,6},{8,15},{9,8},{10,9... | collective-permute-start | bytes 1376264 | tf_op jit(solution)/shard_map/ppermute | solution.py:73
  199.0 28.0 %copy-start.1 = (f32[512,3584]{1,0:T(8,128)S(1)}, f32[512,3584]{1,0:T(8,128)}, u32[]{:S(2)}) copy-start(f32[512,3584]{1,0:T(8,128)} %copy-done) | copy-start | bytes 22020100
  199.0 18.0 %collective-permute-start.16 = (bf16[64,3584]{1,0:T(8,128)(2,1)S(1)}, bf16[64,3584]{1,0:T(8,128)(2,1)S(1)}, u32[]{:S(2)}, u32[]{:S(2)}) collective-permute-start(bf16[64,3584]{1,0:T(8,128)(2,1)S(1)} %get-tuple-element.99), channel_id=1, source_target_pairs={{0,1},{1,2},{2,3},{3,4},{4,5},{5,6},{6,7},{7,0},{8,9},{9,10},{10,1... | collective-permute-start | bytes 1376264 | tf_op jit(solution)/shard_map/ppermute | solution.py:73
  201.4 16.5 %collective-permute-start.17 = (bf16[64,3584]{1,0:T(8,128)(2,1)S(1)}, bf16[64,3584]{1,0:T(8,128)(2,1)S(1)}, u32[]{:S(2)}, u32[]{:S(2)}) collective-permute-start(bf16[64,3584]{1,0:T(8,128)(2,1)S(1)} %get-tuple-element.98), channel_id=1, source_target_pairs={{0,7},{1,0},{2,1},{3,2},{4,3},{5,4},{6,5},{7,6},{8,15},{9,8},{10,9... | collective-permute-start | bytes 1376264 | tf_op jit(solution)/shard_map/ppermute | solution.py:73
  209.7 17.0 %collective-permute-start.30 = (bf16[64,3584]{1,0:T(8,128)(2,1)S(1)}, bf16[64,3584]{1,0:T(8,128)(2,1)S(1)}, u32[]{:S(2)}, u32[]{:S(2)}) collective-permute-start(bf16[64,3584]{1,0:T(8,128)(2,1)S(1)} %get-tuple-element.72), channel_id=1, source_target_pairs={{0,1},{1,2},{2,3},{3,4},{4,5},{5,6},{6,7},{7,0},{8,9},{9,10},{10,1... | collective-permute-start | bytes 1376264 | tf_op jit(solution)/shard_map/ppermute | solution.py:73
  213.6 13.4 %collective-permute-start.31 = (bf16[64,3584]{1,0:T(8,128)(2,1)S(1)}, bf16[64,3584]{1,0:T(8,128)(2,1)S(1)}, u32[]{:S(2)}, u32[]{:S(2)}) collective-permute-start(bf16[64,3584]{1,0:T(8,128)(2,1)S(1)} %get-tuple-element.73), channel_id=1, source_target_pairs={{0,7},{1,0},{2,1},{3,2},{4,3},{5,4},{6,5},{7,6},{8,15},{9,8},{10,9... | collective-permute-start | bytes 1376264 | tf_op jit(solution)/shard_map/ppermute | solution.py:73
  219.5 16.4 %collective-permute-start.18 = (bf16[64,3584]{1,0:T(8,128)(2,1)S(1)}, bf16[64,3584]{1,0:T(8,128)(2,1)S(1)}, u32[]{:S(2)}, u32[]{:S(2)}) collective-permute-start(bf16[64,3584]{1,0:T(8,128)(2,1)S(1)} %get-tuple-element.58), channel_id=1, source_target_pairs={{0,1},{1,2},{2,3},{3,4},{4,5},{5,6},{6,7},{7,0},{8,9},{9,10},{10,1... | collective-permute-start | bytes 1376264 | tf_op jit(solution)/shard_map/ppermute | solution.py:73
  223.2 13.8 %collective-permute-start.19 = (bf16[64,3584]{1,0:T(8,128)(2,1)S(1)}, bf16[64,3584]{1,0:T(8,128)(2,1)S(1)}, u32[]{:S(2)}, u32[]{:S(2)}) collective-permute-start(bf16[64,3584]{1,0:T(8,128)(2,1)S(1)} %get-tuple-element.59), channel_id=1, source_target_pairs={{0,7},{1,0},{2,1},{3,2},{4,3},{5,4},{6,5},{7,6},{8,15},{9,8},{10,9... | collective-permute-start | bytes 1376264 | tf_op jit(solution)/shard_map/ppermute | solution.py:73
  227.2 19.7 %collective-permute-start.33 = (bf16[64,3584]{1,0:T(8,128)(2,1)S(1)}, bf16[64,3584]{1,0:T(8,128)(2,1)S(1)}, u32[]{:S(2)}, u32[]{:S(2)}) collective-permute-start(bf16[64,3584]{1,0:T(8,128)(2,1)S(1)} %get-tuple-element.75), channel_id=1, source_target_pairs={{0,7},{1,0},{2,1},{3,2},{4,3},{5,4},{6,5},{7,6},{8,15},{9,8},{10,9... | collective-permute-start | bytes 1376264 | tf_op jit(solution)/shard_map/ppermute | solution.py:73
  232.5 14.4 %collective-permute-start.32 = (bf16[64,3584]{1,0:T(8,128)(2,1)S(1)}, bf16[64,3584]{1,0:T(8,128)(2,1)S(1)}, u32[]{:S(2)}, u32[]{:S(2)}) collective-permute-start(bf16[64,3584]{1,0:T(8,128)(2,1)S(1)} %get-tuple-element.74), channel_id=1, source_target_pairs={{0,1},{1,2},{2,3},{3,4},{4,5},{5,6},{6,7},{7,0},{8,9},{9,10},{10,1... | collective-permute-start | bytes 1376264 | tf_op jit(solution)/shard_map/ppermute | solution.py:73
  238.6 18.0 %collective-permute-start.21 = (bf16[64,3584]{1,0:T(8,128)(2,1)S(1)}, bf16[64,3584]{1,0:T(8,128)(2,1)S(1)}, u32[]{:S(2)}, u32[]{:S(2)}) collective-permute-start(bf16[64,3584]{1,0:T(8,128)(2,1)S(1)} %get-tuple-element.61), channel_id=1, source_target_pairs={{0,7},{1,0},{2,1},{3,2},{4,3},{5,4},{6,5},{7,6},{8,15},{9,8},{10,9... | collective-permute-start | bytes 1376264 | tf_op jit(solution)/shard_map/ppermute | solution.py:73
  244.0 10.9 %collective-permute-start.20 = (bf16[64,3584]{1,0:T(8,128)(2,1)S(1)}, bf16[64,3584]{1,0:T(8,128)(2,1)S(1)}, u32[]{:S(2)}, u32[]{:S(2)}) collective-permute-start(bf16[64,3584]{1,0:T(8,128)(2,1)S(1)} %get-tuple-element.60), channel_id=1, source_target_pairs={{0,1},{1,2},{2,3},{3,4},{4,5},{5,6},{6,7},{7,0},{8,9},{9,10},{10,1... | collective-permute-start | bytes 1376264 | tf_op jit(solution)/shard_map/ppermute | solution.py:73
  247.0 19.5 %collective-permute-start.34 = (bf16[64,3584]{1,0:T(8,128)(2,1)S(1)}, bf16[64,3584]{1,0:T(8,128)(2,1)S(1)}, u32[]{:S(2)}, u32[]{:S(2)}) collective-permute-start(bf16[64,3584]{1,0:T(8,128)(2,1)S(1)} %dynamic-slice_add_fusion), channel_id=1, source_target_pairs={{0,7},{1,0},{2,1},{3,2},{4,3},{5,4},{6,5},{7,6},{8,15},{9,8},{10,9... | collective-permute-start | bytes 1376264 | tf_op jit(solution)/shard_map/ppermute | solution.py:73
  256.7 14.8 %collective-permute-start.22 = (bf16[64,3584]{1,0:T(8,128)(2,1)S(1)}, bf16[64,3584]{1,0:T(8,128)(2,1)S(1)}, u32[]{:S(2)}, u32[]{:S(2)}) collective-permute-start(bf16[64,3584]{1,0:T(8,128)(2,1)S(1)} %dynamic-slice_add_fusion.5), channel_id=1, source_target_pairs={{0,1},{1,2},{2,3},{3,4},{4,5},{5,6},{6,7},{7,0},{8,9},{9,10},{10,1... | collective-permute-start | bytes 1376264 | tf_op jit(solution)/shard_map/ppermute | solution.py:73
  266.8 20.6 %collective-permute-start.35 = (bf16[64,3584]{1,0:T(8,128)(2,1)S(1)}, bf16[64,3584]{1,0:T(8,128)(2,1)S(1)}, u32[]{:S(2)}, u32[]{:S(2)}) collective-permute-start(bf16[64,3584]{1,0:T(8,128)(2,1)S(1)} %add_convert_fusion), channel_id=1, source_target_pairs={{0,0},{16,32},{32,16},{48,48},{1,1},{17,33},{33,17},{49,49},{2,2},... | collective-permute-start | bytes 1376264 | tf_op jit(solution)/shard_map/ppermute | solution.py:20
  273.0 19.2 %collective-permute-start.23 = (bf16[64,3584]{1,0:T(8,128)(2,1)S(1)}, bf16[64,3584]{1,0:T(8,128)(2,1)S(1)}, u32[]{:S(2)}, u32[]{:S(2)}) collective-permute-start(bf16[64,3584]{1,0:T(8,128)(2,1)S(1)} %add_convert_fusion.1), channel_id=1, source_target_pairs={{0,0},{16,32},{32,16},{48,48},{1,1},{17,33},{33,17},{49,49},{2,2},... | collective-permute-start | bytes 1376264 | tf_op jit(solution)/shard_map/ppermute | solution.py:20
Sparse Core Ops, SparseCore 0:
  59.2 90.7 all-gather.1
